TPU v7x, 512 devices: a whole 4x8x8 slice. The times are simulated.
512 devices in a mesh: dp: 32 (over z_hi, x, core), space: 16 (over y, z_lo).
Axes of the slice: x: 4, y: 8, z: 8 (z_hi: 4, z_lo: 2; z = z_hi * 2 + z_lo), core: 2. Of those that a mesh axis runs over, the one named last changes fastest.
Arguments:
- wake_field: bfloat16 [32, 1, 48, 20, 2304], P('dp', None, 'space'), may hold values from -6 to 6
- spec_weight: bfloat16 [2, 20, 20, 6912], P(None, None, None, 'space'), may hold values from -1.25 to 1.25
- point_weight: bfloat16 [20, 20], replicated, may hold values from -1.25 to 1.25
- bias_term: float32 [20], replicated, may hold values from -3 to 3
- cotangent: bfloat16 [32, 1, 48, 20, 2304], P('dp', None, 'space'), may hold values from -6 to 6
Outputs:
- output_field: bfloat16 [32, 1, 48, 20, 2304], P('dp', None, 'space')
- grad_field: bfloat16 [32, 1, 48, 20, 2304], P('dp', None, 'space')
- grad_spec: float32 [2, 20, 20, 6912], P(None, None, None, 'space')
- grad_point: float32 [20, 20], replicated
- grad_bias: float32 [20], replicated
All inputs are finite; a program needn't handle non-finite values.
Results may differ from a plain program's by a relative error of at most 0.001.
Values sent between devices are 32-bit elements; how exact they have to be, the bound alone decides.
A program may use at most 128 MiB of HBM per device.

v0:
```python
import functools
import math

import jax
import jax.numpy as jnp
import numpy as np
from jax import lax
from jax.experimental import pallas as pl
from jax.experimental.pallas import tpu as pltpu
from jax.sharding import PartitionSpec as P

MESH = pl.DeviceIdType.MESH
F32 = jnp.float32
BF16 = jnp.bfloat16

C = 20
N = 48
MZ = 12
CELLS = N * N
KX = 24
SLABS = 16
PLANES = 3
OWN = 18
MODES = OWN * KX
ROWS = 24
TALL = PLANES * ROWS
TILES = 6
WIDE = TILES * 128


def wave(i):
    return np.where(i < 12, i, i - 24)


def halves(table):
    high = table.astype(np.float32).astype(BF16)
    low = (table - high.astype(np.float64)).astype(np.float32).astype(BF16)
    return np.stack([high, low])


def yz_table():
    lane = np.arange(128)
    g, k, part, q6 = lane // 36, lane % 36 // 12, lane % 12 // 6, lane % 6
    owner = 3 * np.arange(TILES)[:, None] + k[None, :]
    used = (lane < 108)[None, :] & (owner < SLABS)
    q = OWN * owner + 6 * g[None, :] + q6[None, :]
    ky, kz = wave(q // MZ), q % MZ
    cell = np.arange(CELLS)
    y, z = cell // N, cell % N
    phase = (y[:, None, None] * ky[None] + z[:, None, None] * kz[None]) % N
    angle = 2.0 * np.pi * phase / N
    table = np.where(part == 0, np.cos(angle), -np.sin(angle)) / N
    return np.where(used[None], table, 0.0).reshape(CELLS, WIDE)


def x_table():
    lane = np.arange(128)
    k, p, part, q6 = lane // 36, lane % 36 // 12, lane % 12 // 6, lane % 6
    slab = 3 * np.arange(TILES)[:, None] + k[None, :]
    used = ((lane < 108)[None, :] & (slab < SLABS)).reshape(-1)
    x = (PLANES * slab + p[None, :]).reshape(-1)
    part, q6 = np.tile(part, TILES), np.tile(q6, TILES)
    column = np.arange(512)
    part_out, rest = column // 256, column % 256
    q6_out, i = rest // KX, rest % KX
    angle = 2.0 * np.pi * (x[:, None] * wave(i)[None, :] % N) / N
    cosine, sine = np.cos(angle), np.sin(angle)
    same = part[:, None] == part_out[None, :]
    table = np.where(same, cosine, np.where(part[:, None] == 1, sine, -sine)) / math.sqrt(N)
    keep = used[:, None] & (rest < 6 * KX)[None, :] & (q6[:, None] == q6_out[None, :])
    return np.where(keep, table, 0.0)


@functools.cache
def tables():
    yz, x = yz_table(), x_table()
    yz_two, x_two = halves(yz), halves(x)
    forward = np.ascontiguousarray(yz_two.reshape(2, CELLS, 3, 256).transpose(2, 0, 1, 3))
    inverse = np.ascontiguousarray(yz_two.transpose(0, 2, 1).reshape(2, WIDE, 9, 256).transpose(2, 0, 1, 3))
    x_inverse = np.ascontiguousarray(x_two.transpose(0, 2, 1))
    own = np.arange(512) // KX
    weight = np.stack([np.where((6 * parity + own) % MZ == 0, 1.0, 2.0) for parity in range(2)])
    weight = np.broadcast_to(weight[:, None, :], (2, 8, 512)).astype(np.float32)
    return forward, inverse, x_two, x_inverse, np.ascontiguousarray(weight)


def times(value, high, low):
    rows = value.shape[0]
    top = value.astype(BF16)
    wide = top.astype(F32)
    both = jnp.concatenate([wide, value - wide], axis=0).astype(BF16)
    first = jnp.dot(both, high, preferred_element_type=F32)
    return first[:rows] + first[rows:] + jnp.dot(top, low, preferred_element_type=F32)


def kernel(
    wake_hbm, cot_hbm, weight_hbm, small, kz_weight, fwd_hbm, inv_hbm, x_hbm, xt_hbm,
    out_hbm, grad_hbm, spec_hbm, sums_ref,
    wake, cot, weight, fwd, inv, xf, xt,
    values, spectra, slab, grads, lined, pieces, modes, mixed, grad_modes,
    send, recv, all_modes, all_grads, partial, landed, gathered, sums8, sums4,
    out_vmem, grad_vmem,
    load_sem, store_sem, send_sem, recv_sem, dp_send, dp_recv,
):
    dp = lax.axis_index("dp")
    me = lax.axis_index("space")
    z_hi, eight = dp // 8, dp % 8
    x_pos, core = eight // 2, eight % 2
    lane = lax.broadcasted_iota(jnp.int32, (C, 128), 1)
    third = lane // 36
    slot = jnp.where(lane < 108, lane % 36 // 12, 3)

    loads = [
        pltpu.make_async_copy(wake_hbm, wake, load_sem.at[0]),
        pltpu.make_async_copy(fwd_hbm.at[0], fwd.at[0], load_sem.at[1]),
        pltpu.make_async_copy(fwd_hbm.at[1], fwd.at[1], load_sem.at[2]),
        pltpu.make_async_copy(fwd_hbm.at[2], fwd.at[2], load_sem.at[3]),
        pltpu.make_async_copy(x_hbm, xf, load_sem.at[4]),
        pltpu.make_async_copy(weight_hbm, weight, load_sem.at[5]),
        pltpu.make_async_copy(xt_hbm, xt, load_sem.at[6]),
        pltpu.make_async_copy(inv_hbm, inv, load_sem.at[7]),
        pltpu.make_async_copy(cot_hbm, cot, load_sem.at[8]),
    ]
    for load in loads:
        load.start()

    barrier = pltpu.get_barrier_semaphore()
    for r in range(1, 16):
        pl.semaphore_signal(barrier, inc=1, device_id=(dp, (me + r) % 16), device_id_type=MESH)
    for r in range(1, 8):
        peer = z_hi * 8 + (eight + r) % 8
        pl.semaphore_signal(barrier, inc=1, device_id=(peer, me), device_id_type=MESH)
    for r in range(1, 4):
        peer = (z_hi + r) % 4 * 8 + eight
        pl.semaphore_signal(barrier, inc=1, device_id=(peer, me), device_id_type=MESH)

    values[...] = jnp.zeros((TALL, CELLS), F32)
    lined[...] = jnp.zeros((TALL, WIDE), F32)
    pieces[...] = jnp.zeros((TALL, 512), F32)
    mixed[...] = jnp.zeros((2, C, 512), F32)
    loads[0].wait()
    for p in range(PLANES):
        values[ROWS * p : ROWS * p + C, :] = wake[0, 0, p].astype(F32)

    def space_copy(phase, r):
        to = (me + r) % 16
        return pltpu.make_async_remote_copy(
            src_ref=send.at[phase, to], dst_ref=recv.at[phase, me],
            send_sem=send_sem.at[phase, r], recv_sem=recv_sem.at[phase, r],
            device_id=(dp, to), device_id_type=MESH,
        )

    def space_start(phase):
        for r in range(1, 16):
            space_copy(phase, r).start()
        recv[phase, me] = send[phase, me]

    def space_wait(phase):
        for r in range(1, 16):
            space_copy(phase, r).wait()

    def turn(value, shift):
        shift %= 128
        return value if shift == 0 else pltpu.roll(value, shift, 1)

    def choose(where, parts):
        total = jnp.zeros((C, 128), F32)
        for index, part in parts:
            total = jnp.where(where == index, part, total)
        return total

    def slab_to_owners(phase, ride):
        for t in range(TILES):
            held = [spectra[ROWS * p : ROWS * p + C, 128 * t : 128 * t + 128] for p in range(PLANES)]
            for k in range(3):
                if 3 * t + k < SLABS:
                    message = choose(slot, [(p, turn(held[p], 12 * (p - k))) for p in range(PLANES)])
                    send[phase, 3 * t + k] = message if ride is None else message + ride

    def owners_to_slab(phase):
        for t in range(TILES):
            ks = [k for k in range(3) if 3 * t + k < SLABS]
            held = [recv[phase, 3 * t + k] for k in ks]
            for p in range(PLANES):
                lined[ROWS * p : ROWS * p + C, 128 * t : 128 * t + 128] = choose(
                    slot, [(k, turn(held[k], 12 * (k - p))) for k in ks]
                )

    def line_up_planes(phase):
        for u in range(TILES):
            ks = [k for k in range(3) if 3 * u + k < SLABS]
            held = [recv[phase, 3 * u + k] for k in ks]
            for g in range(3):
                lined[ROWS * g : ROWS * g + C, 128 * u : 128 * u + 128] = choose(
                    third, [(k, turn(held[k], 36 * (k - g))) for k in ks]
                )

    def planes_to_slabs(phase, ride):
        for u in range(TILES):
            held = [slab[ROWS * g : ROWS * g + C, 128 * u : 128 * u + 128] for g in range(3)]
            for k in range(3):
                if 3 * u + k < SLABS:
                    message = choose(third, [(g, turn(held[g], 36 * (g - k))) for g in range(3)])
                    send[phase, 3 * u + k] = message if ride is None else message + ride

    def along_x(target, scale):
        result = times(lined[...], xf[0], xf[1])
        for part in range(2):
            block = [result[ROWS * g : ROWS * g + ROWS, 256 * part : 256 * part + 256] for g in range(3)]
            second, last = pltpu.roll(block[1], 16, 1), pltpu.roll(block[2], 32, 1)
            strips = [
                block[0][:, :128],
                block[0][:, 128:] + second[:, :128],
                second[:, 128:] + last[:, :128],
                last[:, 128:],
            ]
            for j in range(4):
                strip = strips[j][:C]
                if scale is not None:
                    strip = strip * scale[:, 128 * j : 128 * j + 128]
                target[part, :, 128 * j : 128 * j + 128] = strip

    def back_along_x():
        for part in range(2):
            full = mixed[part]
            pieces[0:C, 256 * part : 256 * part + 256] = full[:, :256]
            pieces[ROWS : ROWS + C, 256 * part : 256 * part + 256] = pltpu.roll(full, 512 - 144, 1)[:, :256]
            pieces[2 * ROWS : 2 * ROWS + C, 256 * part : 256 * part + 256] = pltpu.roll(full, 512 - 288, 1)[:, :256]
        slab[...] = times(pieces[...], xt[0], xt[1])

    def gather_copy(kind, source, target, r):
        to = (eight + r) % 8
        return pltpu.make_async_remote_copy(
            src_ref=source.at[:, :, pl.ds(pl.multiple_of(to // 2 * 128, 128), 128)],
            dst_ref=target.at[eight],
            send_sem=dp_send.at[kind, r], recv_sem=dp_recv.at[kind, r],
            device_id=(z_hi * 8 + to, me), device_id_type=MESH,
        )

    def gather_start(kind, source, target):
        for r in range(1, 8):
            gather_copy(kind, source, target, r).start()
        target[eight] = source[:, :, pl.ds(pl.multiple_of(x_pos * 128, 128), 128)]

    tall = values[...].astype(BF16)
    for n in range(3):
        loads[1 + n].wait()
        spectra[:, 256 * n : 256 * n + 256] = jnp.dot(
            tall, fwd[n, 0], preferred_element_type=F32
        ) + jnp.dot(tall, fwd[n, 1], preferred_element_type=F32)
    slab_to_owners(0, None)
    pl.semaphore_wait(barrier, 25)
    space_start(0)
    for load in loads[4:]:
        load.wait()
    space_wait(0)
    line_up_planes(0)
    along_x(modes, None)
    gather_start(0, modes, all_modes)

    row = kz_weight[me % 2, 0:1, :]

    def mix_step(c, carry):
        real, imag = carry
        w_real, w_imag = weight[0, c].astype(F32), weight[1, c].astype(F32)
        m_real, m_imag = modes[0, pl.ds(c, 1), :MODES], modes[1, pl.ds(c, 1), :MODES]
        real = real + w_real * m_real - w_imag * m_imag
        imag = imag + w_real * m_imag + w_imag * m_real
        return real, imag

    nothing = jnp.zeros((C, MODES), F32)
    real, imag = lax.fori_loop(0, C, mix_step, (nothing, nothing))
    mixed[0, :, :MODES] = real * row[:, :MODES]
    mixed[1, :, :MODES] = imag * row[:, :MODES]
    back_along_x()
    planes_to_slabs(1, None)
    space_start(1)

    def diagonal(matrix):
        return jnp.concatenate([turn(matrix, ROWS * p) for p in range(PLANES)], axis=0)[:, :TALL].astype(BF16)

    to_out, to_in = diagonal(small[0]), diagonal(small[1])
    bias = jnp.concatenate([small[2]] * PLANES, axis=0)[:, 0:1]
    channel = lax.broadcasted_iota(jnp.int32, (TALL, 256), 0) % ROWS
    space_wait(1)
    owners_to_slab(1)

    full = lined[...]
    rate = math.sqrt(2.0 / math.pi)
    bias_sum = jnp.zeros((TALL, 1), F32)
    for n in range(9):
        columns = slice(256 * n, 256 * n + 256)
        pre = times(full, inv[n, 0], inv[n, 1])
        pre = pre + jnp.dot(to_out, values[:, columns].astype(BF16), preferred_element_type=F32) + bias
        square = pre * pre
        bend = jnp.tanh(rate * (pre + 0.044715 * (square * pre)))
        half = 0.5 * (1.0 + bend)
        slope = half + 0.5 * pre * (1.0 - bend * bend) * (rate * (1.0 + 3 * 0.044715 * square))
        active = half * pre
        for p in range(PLANES):
            out_vmem[0, 0, p, :, columns] = active[ROWS * p : ROWS * p + C].astype(BF16)
            grads[ROWS * p : ROWS * p + C, columns] = slope[ROWS * p : ROWS * p + C] * cot[0, 0, p, :, columns].astype(F32)
            grads[ROWS * p + C : ROWS * p + ROWS, columns] = jnp.zeros((ROWS - C, 256), F32)
        bias_sum = bias_sum + jnp.sum(grads[:, columns], axis=1, keepdims=True)
    store_out = pltpu.make_async_copy(out_vmem, out_hbm, store_sem.at[0])
    store_out.start()

    full = grads[...]
    for n in range(3):
        spectra[:, 256 * n : 256 * n + 256] = times(full, fwd[n, 0], fwd[n, 1])
    bias_own = bias_sum[:C] + bias_sum[ROWS : ROWS + C] + bias_sum[2 * ROWS : 2 * ROWS + C]
    slab_to_owners(2, jnp.where(lane == 108, bias_own, 0.0))
    space_start(2)

    point = jnp.zeros((ROWS, ROWS), F32)
    last = (((1,), (1,)), ((), ()))
    for p in range(PLANES):
        field = values[ROWS * p : ROWS * p + ROWS, :].astype(BF16)
        slope = grads[ROWS * p : ROWS * p + ROWS, :]
        high = slope.astype(BF16)
        low = (slope - high.astype(F32)).astype(BF16)
        point = point + lax.dot_general(field, high, last, preferred_element_type=F32)
        point = point + lax.dot_general(field, low, last, preferred_element_type=F32)
    point = jnp.concatenate([point[:C], jnp.zeros((C, 128 - ROWS), F32)], axis=1)
    point = jnp.where(lane >= 108, turn(point, 108), 0.0)
    for n in range(9):
        columns = slice(256 * n, 256 * n + 256)
        slope = grads[:, columns]
        high = slope.astype(BF16)
        low = (slope - high.astype(F32)).astype(BF16)
        values[:, columns] = jnp.dot(to_in, high, preferred_element_type=F32) + jnp.dot(
            to_in, low, preferred_element_type=F32
        )

    space_wait(2)
    line_up_planes(2)
    along_x(grad_modes, row)
    gather_start(1, grad_modes, all_grads)

    def grad_step(c, carry):
        w_real, w_imag = weight[0, c].astype(F32), weight[1, c].astype(F32)
        g_real, g_imag = grad_modes[0, :, :MODES], grad_modes[1, :, :MODES]
        mixed[0, pl.ds(c, 1), :MODES] = jnp.sum(w_real * g_real + w_imag * g_imag, axis=0, keepdims=True)
        mixed[1, pl.ds(c, 1), :MODES] = jnp.sum(w_real * g_imag - w_imag * g_real, axis=0, keepdims=True)
        return carry

    lax.fori_loop(0, C, grad_step, 0)
    back_along_x()
    planes_to_slabs(3, point)
    space_start(3)

    for r in range(1, 8):
        gather_copy(0, modes, all_modes, r).wait()
        gather_copy(1, grad_modes, all_grads, r).wait()

    def part_step(c, carry):
        total = jnp.zeros((C, 128), F32)
        for b in range(8):
            g_real, g_imag = all_grads[b, 0], all_grads[b, 1]
            first = jnp.where(core == 0, g_real, g_imag)
            second = jnp.where(core == 0, g_imag, -g_real)
            total = total + all_modes[b, 0, pl.ds(c, 1), :] * first + all_modes[b, 1, pl.ds(c, 1), :] * second
        partial[c] = total
        return carry

    lax.fori_loop(0, C, part_step, 0)

    def scatter_copy(r):
        to = (z_hi + r) % 4
        return pltpu.make_async_remote_copy(
            src_ref=partial.at[pl.ds(to * 5, 5)], dst_ref=landed.at[r - 1],
            send_sem=dp_send.at[2, r], recv_sem=dp_recv.at[2, r],
            device_id=(to * 8 + eight, me), device_id_type=MESH,
        )

    for r in range(1, 4):
        scatter_copy(r).start()

    bias_total = jnp.zeros((C, 128), F32)
    for s in range(SLABS):
        bias_total = bias_total + recv[2, s]
    space_wait(3)
    owners_to_slab(3)
    point_total = jnp.zeros((C, 128), F32)
    for s in range(SLABS):
        point_total = point_total + recv[3, s]
    small_sum = jnp.where(lane >= 108, point_total, jnp.where(lane == 0, turn(bias_total, 20), 0.0))
    sums8[eight] = small_sum

    def eight_copy(r):
        to = (eight + r) % 8
        return pltpu.make_async_remote_copy(
            src_ref=sums8.at[eight], dst_ref=sums8.at[eight],
            send_sem=dp_send.at[3, r], recv_sem=dp_recv.at[3, r],
            device_id=(z_hi * 8 + to, me), device_id_type=MESH,
        )

    for r in range(1, 8):
        eight_copy(r).start()

    for r in range(1, 4):
        scatter_copy(r).wait()
    for j in range(5):
        gathered[x_pos, core, z_hi * 5 + j] = (
            partial[z_hi * 5 + j] + landed[0, j] + landed[1, j] + landed[2, j]
        )

    def z_copy(r):
        to = (z_hi + r) % 4
        block = gathered.at[x_pos, core, pl.ds(z_hi * 5, 5)]
        return pltpu.make_async_remote_copy(
            src_ref=block, dst_ref=block,
            send_sem=dp_send.at[4, r], recv_sem=dp_recv.at[4, r],
            device_id=(to * 8 + eight, me), device_id_type=MESH,
        )

    for r in range(1, 4):
        z_copy(r).start()

    full = lined[...]
    for n in range(9):
        columns = slice(256 * n, 256 * n + 256)
        result = times(full, inv[n, 0], inv[n, 1]) + values[:, columns]
        for p in range(PLANES):
            grad_vmem[0, 0, p, :, columns] = result[ROWS * p : ROWS * p + C].astype(BF16)
    store_grad = pltpu.make_async_copy(grad_vmem, grad_hbm, store_sem.at[1])
    store_grad.start()

    for r in range(1, 8):
        eight_copy(r).wait()
    total = sums8[0]
    for b in range(1, 8):
        total = total + sums8[b]
    sums4[z_hi] = total

    def four_copy(r):
        to = (z_hi + r) % 4
        return pltpu.make_async_remote_copy(
            src_ref=sums4.at[z_hi], dst_ref=sums4.at[z_hi],
            send_sem=dp_send.at[5, r], recv_sem=dp_recv.at[5, r],
            device_id=(to * 8 + eight, me), device_id_type=MESH,
        )

    for r in range(1, 4):
        four_copy(r).start()

    for r in range(1, 4):
        z_copy(r).wait()

    def x_copy(r):
        to = (x_pos + r) % 4
        block = gathered.at[x_pos, core]
        return pltpu.make_async_remote_copy(
            src_ref=block, dst_ref=block,
            send_sem=dp_send.at[6, r], recv_sem=dp_recv.at[6, r],
            device_id=(z_hi * 8 + to * 2 + core, me), device_id_type=MESH,
        )

    def core_copy(r):
        block = gathered.at[(x_pos - r) % 4, core]
        return pltpu.make_async_remote_copy(
            src_ref=block, dst_ref=block,
            send_sem=dp_send.at[7, r], recv_sem=dp_recv.at[7, r],
            device_id=(z_hi * 8 + x_pos * 2 + 1 - core, me), device_id_type=MESH,
        )

    def strip_store(r, part):
        strip = (x_pos - r) % 4
        return pltpu.make_async_copy(
            gathered.at[strip, part],
            spec_hbm.at[part, :, :, pl.ds(pl.multiple_of(strip * 128, 128), 128)],
            store_sem.at[2 + 2 * r + (part != core).astype(jnp.int32)],
        )

    for r in range(1, 4):
        x_copy(r).start()
    core_copy(0).start()
    strip_store(0, core).start()
    for r in (1, 3, 2):
        x_copy(r).wait_recv()
        core_copy(r).start()
        strip_store(r, core).start()
    for r in range(1, 4):
        four_copy(r).wait()
    sums_ref[...] = sums4[0] + sums4[1] + sums4[2] + sums4[3]
    for r in (0, 1, 3, 2):
        core_copy(r).wait()
        strip_store(r, 1 - core).start()
    for r in range(1, 4):
        x_copy(r).wait_send()
    for r in range(4):
        strip_store(r, core).wait()
        strip_store(r, 1 - core).wait()
    store_out.wait()
    store_grad.wait()


def on_device(wake_field, spec_weight, point_weight, bias_term, cotangent):
    forward, inverse, x_two, x_inverse, kz_weight = tables()
    matrix = point_weight.astype(F32)
    small = jnp.stack([
        jnp.pad(matrix.T, ((0, ROWS - C), (0, 128 - C))),
        jnp.pad(matrix, ((0, ROWS - C), (0, 128 - C))),
        jnp.pad(jnp.broadcast_to(bias_term[:, None], (C, 128)), ((0, ROWS - C), (0, 0))),
    ])
    anywhere = pl.BlockSpec(memory_space=pl.ANY)
    inside = pl.BlockSpec(memory_space=pltpu.VMEM)
    field = wake_field.shape
    output_field, grad_field, grad_spec, sums = pl.pallas_call(
        kernel,
        out_shape=(
            jax.ShapeDtypeStruct(field, BF16),
            jax.ShapeDtypeStruct(field, BF16),
            jax.ShapeDtypeStruct((2, C, C, 512), F32),
            jax.ShapeDtypeStruct((C, 128), F32),
        ),
        in_specs=[anywhere, anywhere, anywhere, inside, inside, anywhere, anywhere, anywhere, anywhere],
        out_specs=(anywhere, anywhere, anywhere, inside),
        scratch_shapes=[
            pltpu.VMEM(field, BF16),
            pltpu.VMEM(field, BF16),
            pltpu.VMEM(spec_weight.shape, BF16),
            pltpu.VMEM(forward.shape, BF16),
            pltpu.VMEM(inverse.shape, BF16),
            pltpu.VMEM(x_two.shape, BF16),
            pltpu.VMEM(x_inverse.shape, BF16),
            pltpu.VMEM((TALL, CELLS), F32),
            pltpu.VMEM((TALL, WIDE), F32),
            pltpu.VMEM((TALL, WIDE), F32),
            pltpu.VMEM((TALL, CELLS), F32),
            pltpu.VMEM((TALL, WIDE), F32),
            pltpu.VMEM((TALL, 512), F32),
            pltpu.VMEM((2, C, 512), F32),
            pltpu.VMEM((2, C, 512), F32),
            pltpu.VMEM((2, C, 512), F32),
            pltpu.VMEM((4, SLABS, C, 128), F32),
            pltpu.VMEM((4, SLABS, C, 128), F32),
            pltpu.VMEM((8, 2, C, 128), F32),
            pltpu.VMEM((8, 2, C, 128), F32),
            pltpu.VMEM((C, C, 128), F32),
            pltpu.VMEM((3, 5, C, 128), F32),
            pltpu.VMEM((4, 2, C, C, 128), F32),
            pltpu.VMEM((8, C, 128), F32),
            pltpu.VMEM((4, C, 128), F32),
            pltpu.VMEM(field, BF16),
            pltpu.VMEM(field, BF16),
            pltpu.SemaphoreType.DMA((9,)),
            pltpu.SemaphoreType.DMA((10,)),
            pltpu.SemaphoreType.DMA((4, 16)),
            pltpu.SemaphoreType.DMA((4, 16)),
            pltpu.SemaphoreType.DMA((8, 8)),
            pltpu.SemaphoreType.DMA((8, 8)),
        ],
        compiler_params=pltpu.CompilerParams(
            collective_id=0, has_side_effects=True, vmem_limit_bytes=56 * 1024 * 1024
        ),
    )(wake_field, cotangent, spec_weight, small, kz_weight, forward, inverse, x_two, x_inverse)
    return (
        output_field,
        grad_field,
        grad_spec[..., :MODES],
        sums[:, 108:128],
        sums[:, 0],
    )


def solution(mesh):
    placed = (
        P("dp", None, "space", None, None),
        P(None, None, None, "space"),
        P(),
        P(),
        P("dp", None, "space", None, None),
    )
    return jax.shard_map(
        on_device,
        mesh=mesh,
        in_specs=placed,
        out_specs=(
            P("dp", None, "space", None, None),
            P("dp", None, "space", None, None),
            P(None, None, None, "space"),
            P(),
            P(),
        ),
        check_vma=False,
    )
```

profile of v0, /device:TPU:1, one launch (start us, length us, event | category | flops | bytes accessed | tf_op | source)
XLA Modules:
  0.0 90.4 jit_solution(5161771853570210709)
XLA Ops:
  0.6 2.2 %copy.19.weight_hbm = bf16[2,20,20,432]{3,2,1,0:T(8,128)(2,1)} copy(bf16[2,20,20,432]{3,0,2,1:T(2,128)(2,1)} %param.11) | data formatting | bytes 1382400 | tf_op args[1]
  2.9 0.7 pad.13
  3.5 0.1 stack.14
  3.6 0.7 convert_bitcast_fusion
  4.3 0.1 copy.18
  4.4 0.6 pad_maximum_fusion.small
  5.0 78.5 %shard_map.137 = (bf16[1,1,3,20,2304]{4,3,2,1,0:T(8,128)(2,1)}, bf16[1,1,3,20,2304]{4,3,2,1,0:T(8,128)(2,1)}, f32[2,20,20,512]{3,2,1,0:T(8,128)}, f32[20,128]{1,0:T(8,128)}) custom-call(bf16[1,1,3,20,2304]{4,3,2,1,0:T(8,128)(2,1)} %wake_hbm.1, bf16[1,1,3,20,2304]{4,3,2,1,0:T(8,128)(2,1)} %cot_hbm.1, bf16[2,20,20,432]{3,2,1,0:T(8,128)(2,1)} %copy.19.weight_hbm, ...), custom_call_target="tpu_custom_call" | custom-call | tf_op jit(solution)/shard_map/pallas_call | solution.py:509
  83.5 0.0 copy-start.2
  83.5 0.0 copy-start.1
  83.5 0.0 copy-start
  83.6 4.0 %copy.20 = f32[2,20,20,432]{3,0,2,1:T(2,128)} copy(f32[2,20,20,432]{3,2,1,0:T(8,128)} %bitcast.7) | data formatting | bytes 2764800
  87.6 0.0 copy-done.2
  87.6 0.7 slice.10
  88.3 0.6 slice_reduce_fusion
  88.9 0.0 copy-done.1
  88.9 0.7 copy.23
  89.6 0.0 copy-done
  89.6 0.7 copy.24
  (2 shorter events, 0.0 us)
Async XLA Ops:
  83.5 4.1 %copy-start.2 = (f32[20,128]{1,0:T(8,128)S(1)}, f32[20,128]{1,0:T(8,128)}, u32[]{:S(2)}) copy-start(f32[20,128]{1,0:T(8,128)} %get-tuple-element.12) | copy-start | bytes 30724
  83.5 5.4 %copy-start.1 = (bf16[1,1,3,20,2304]{4,3,2,1,0:T(8,128)(2,1)S(1)}, bf16[1,1,3,20,2304]{4,3,2,1,0:T(8,128)(2,1)}, u32[]{:S(2)}) copy-start(bf16[1,1,3,20,2304]{4,3,2,1,0:T(8,128)(2,1)} %get-tuple-element.30) | copy-start | bytes 829444
  83.5 6.1 %copy-start = (bf16[1,1,3,20,2304]{4,3,2,1,0:T(8,128)(2,1)S(1)}, bf16[1,1,3,20,2304]{4,3,2,1,0:T(8,128)(2,1)}, u32[]{:S(2)}) copy-start(bf16[1,1,3,20,2304]{4,3,2,1,0:T(8,128)(2,1)} %get-tuple-element.31) | copy-start | bytes 829444
where the time goes:
time: 90.7 us; the launch traced here: 90.4 us
  Pallas kernels  78.5 us (87%)
  local copies, waits for them, and re-layouts  9.84 us (11%)
  other arithmetic  1.34 us (1%)
    pallas_call x1, Pallas kernels, on_device(): pl.pallas_call(kernel, out_shape=(jax.ShapeDtypeStruct(field, BF16), jax....  78.5 us
    unnamed x10, local copies, waits for them, and re-layouts  7.75 us

commit v1 on v0

--- a/solution.py
+++ b/solution.py
@@ -26,6 +26,7 @@
 TALL = PLANES * ROWS
 TILES = 6
 WIDE = TILES * 128
+PAIRS = 2 * C
 
 
 def wave(i):
@@ -94,13 +95,13 @@
 
 
 def kernel(
-    wake_hbm, cot_hbm, weight_hbm, small, kz_weight, fwd_hbm, inv_hbm, x_hbm, xt_hbm,
+    wake_hbm, cot_hbm, weight_hbm, point_weight, bias_term, kz_weight, fwd_hbm, inv_hbm, x_hbm, xt_hbm,
     out_hbm, grad_hbm, spec_hbm, sums_ref,
     wake, cot, weight, fwd, inv, xf, xt,
-    values, spectra, slab, grads, lined, pieces, modes, mixed, grad_modes,
+    values, slopes, maps, spectra, slab, grads, lined, pieces, modes, mixed, grad_modes, matrix,
     send, recv, all_modes, all_grads, partial, landed, gathered, sums8, sums4,
     out_vmem, grad_vmem,
-    load_sem, store_sem, send_sem, recv_sem, dp_send, dp_recv,
+    load_sem, store_sem, spec_sem, send_sem, recv_sem, dp_send, dp_recv, x_send, x_recv,
 ):
     dp = lax.axis_index("dp")
     me = lax.axis_index("space")
@@ -109,19 +110,20 @@
     lane = lax.broadcasted_iota(jnp.int32, (C, 128), 1)
     third = lane // 36
     slot = jnp.where(lane < 108, lane % 36 // 12, 3)
+    even = lax.broadcasted_iota(jnp.int32, (PAIRS, 128), 0) % 2 == 0
 
     loads = [
         pltpu.make_async_copy(wake_hbm, wake, load_sem.at[0]),
         pltpu.make_async_copy(fwd_hbm.at[0], fwd.at[0], load_sem.at[1]),
         pltpu.make_async_copy(fwd_hbm.at[1], fwd.at[1], load_sem.at[2]),
         pltpu.make_async_copy(fwd_hbm.at[2], fwd.at[2], load_sem.at[3]),
-        pltpu.make_async_copy(x_hbm, xf, load_sem.at[4]),
-        pltpu.make_async_copy(weight_hbm, weight, load_sem.at[5]),
-        pltpu.make_async_copy(xt_hbm, xt, load_sem.at[6]),
-        pltpu.make_async_copy(inv_hbm, inv, load_sem.at[7]),
-        pltpu.make_async_copy(cot_hbm, cot, load_sem.at[8]),
+        pltpu.make_async_copy(weight_hbm, weight, load_sem.at[4]),
+        pltpu.make_async_copy(cot_hbm, cot, load_sem.at[5]),
+        pltpu.make_async_copy(x_hbm, xf, load_sem.at[6]),
+        pltpu.make_async_copy(xt_hbm, xt, load_sem.at[7]),
+        pltpu.make_async_copy(inv_hbm, inv, load_sem.at[8]),
     ]
-    for load in loads:
+    for load in loads[:4]:
         load.start()
 
     barrier = pltpu.get_barrier_semaphore()
@@ -136,8 +138,6 @@
 
     values[...] = jnp.zeros((TALL, CELLS), F32)
     lined[...] = jnp.zeros((TALL, WIDE), F32)
-    pieces[...] = jnp.zeros((TALL, 512), F32)
-    mixed[...] = jnp.zeros((2, C, 512), F32)
     loads[0].wait()
     for p in range(PLANES):
         values[ROWS * p : ROWS * p + C, :] = wake[0, 0, p].astype(F32)
@@ -162,6 +162,9 @@
     def turn(value, shift):
         shift %= 128
         return value if shift == 0 else pltpu.roll(value, shift, 1)
+
+    def other(value):
+        return jnp.where(even, pltpu.roll(value, PAIRS - 1, 0), -pltpu.roll(value, 1, 0))
 
     def choose(where, parts):
         total = jnp.zeros((C, 128), F32)
@@ -218,21 +221,24 @@
                 strip = strips[j][:C]
                 if scale is not None:
                     strip = strip * scale[:, 128 * j : 128 * j + 128]
-                target[part, :, 128 * j : 128 * j + 128] = strip
+                target[j, pl.ds(part, C, stride=2), :] = strip
 
     def back_along_x():
         for part in range(2):
-            full = mixed[part]
+            strips = [mixed[j, pl.ds(part, C, stride=2), :] for j in range(4)]
+            full = jnp.concatenate(strips, axis=1)
             pieces[0:C, 256 * part : 256 * part + 256] = full[:, :256]
             pieces[ROWS : ROWS + C, 256 * part : 256 * part + 256] = pltpu.roll(full, 512 - 144, 1)[:, :256]
             pieces[2 * ROWS : 2 * ROWS + C, 256 * part : 256 * part + 256] = pltpu.roll(full, 512 - 288, 1)[:, :256]
         slab[...] = times(pieces[...], xt[0], xt[1])
 
+    def strip_at(index):
+        return pl.ds(pl.multiple_of(index * 128, 128), 128)
+
     def gather_copy(kind, source, target, r):
         to = (eight + r) % 8
         return pltpu.make_async_remote_copy(
-            src_ref=source.at[:, :, pl.ds(pl.multiple_of(to // 2 * 128, 128), 128)],
-            dst_ref=target.at[eight],
+            src_ref=source.at[to // 2], dst_ref=target.at[eight],
             send_sem=dp_send.at[kind, r], recv_sem=dp_recv.at[kind, r],
             device_id=(z_hi * 8 + to, me), device_id_type=MESH,
         )
@@ -240,7 +246,7 @@
     def gather_start(kind, source, target):
         for r in range(1, 8):
             gather_copy(kind, source, target, r).start()
-        target[eight] = source[:, :, pl.ds(pl.multiple_of(x_pos * 128, 128), 128)]
+        target[eight] = source[x_pos]
 
     tall = values[...].astype(BF16)
     for n in range(3):
@@ -248,40 +254,60 @@
         spectra[:, 256 * n : 256 * n + 256] = jnp.dot(
             tall, fwd[n, 0], preferred_element_type=F32
         ) + jnp.dot(tall, fwd[n, 1], preferred_element_type=F32)
+    for load in loads[4:]:
+        load.start()
     slab_to_owners(0, None)
     pl.semaphore_wait(barrier, 25)
     space_start(0)
-    for load in loads[4:]:
+
+    pieces[...] = jnp.zeros((TALL, 512), F32)
+    maps[:, :, 384:] = jnp.zeros((C, PAIRS, 128), F32)
+    matrix[...] = jnp.zeros((ROWS, 128), F32)
+    slopes[...] = jnp.zeros((TALL, CELLS), F32)
+    matrix[0:C, 0:C] = point_weight[...].astype(F32)
+    loads[4].wait()
+
+    def cast_step(c, carry):
+        maps[c, :, :MODES] = weight[c].astype(F32).reshape(PAIRS, MODES)
+        return carry
+
+    lax.fori_loop(0, C, cast_step, 0)
+    loads[5].wait()
+    for p in range(PLANES):
+        slopes[ROWS * p : ROWS * p + C, :] = cot[0, 0, p].astype(F32)
+    for load in loads[6:]:
         load.wait()
+
     space_wait(0)
     line_up_planes(0)
     along_x(modes, None)
     gather_start(0, modes, all_modes)
-
     row = kz_weight[me % 2, 0:1, :]
 
-    def mix_step(c, carry):
-        real, imag = carry
-        w_real, w_imag = weight[0, c].astype(F32), weight[1, c].astype(F32)
-        m_real, m_imag = modes[0, pl.ds(c, 1), :MODES], modes[1, pl.ds(c, 1), :MODES]
-        real = real + w_real * m_real - w_imag * m_imag
-        imag = imag + w_real * m_imag + w_imag * m_real
-        return real, imag
-
-    nothing = jnp.zeros((C, MODES), F32)
-    real, imag = lax.fori_loop(0, C, mix_step, (nothing, nothing))
-    mixed[0, :, :MODES] = real * row[:, :MODES]
-    mixed[1, :, :MODES] = imag * row[:, :MODES]
+    def mix_step(j, carry):
+        strip = strip_at(j)
+        first, second = jnp.zeros((PAIRS, 128), F32), jnp.zeros((PAIRS, 128), F32)
+        for c in range(C):
+            weights = maps[c, :, strip]
+            first = first + weights * modes[j, 2 * c : 2 * c + 1, :]
+            second = second + weights * modes[j, 2 * c + 1 : 2 * c + 2, :]
+        mixed[j] = (first - other(second)) * kz_weight[me % 2, 0:1, strip]
+        return carry
+
+    lax.fori_loop(0, 4, mix_step, 0)
     back_along_x()
     planes_to_slabs(1, None)
     space_start(1)
 
-    def diagonal(matrix):
-        return jnp.concatenate([turn(matrix, ROWS * p) for p in range(PLANES)], axis=0)[:, :TALL].astype(BF16)
-
-    to_out, to_in = diagonal(small[0]), diagonal(small[1])
-    bias = jnp.concatenate([small[2]] * PLANES, axis=0)[:, 0:1]
-    channel = lax.broadcasted_iota(jnp.int32, (TALL, 256), 0) % ROWS
+    to_in = jnp.concatenate([turn(matrix[...], ROWS * p) for p in range(PLANES)], axis=0)[:, :TALL].astype(BF16)
+    here = lax.broadcasted_iota(jnp.int32, (ROWS, C), 0) == lax.broadcasted_iota(jnp.int32, (ROWS, C), 1)
+    bias = jnp.sum(jnp.where(here, bias_term[...], 0.0), axis=1, keepdims=True)
+    bias = jnp.concatenate([bias] * PLANES, axis=0)
+    for n in range(9):
+        columns = slice(256 * n, 256 * n + 256)
+        grads[:, columns] = bias + lax.dot_general(
+            to_in, values[:, columns].astype(BF16), (((0,), (0,)), ((), ())), preferred_element_type=F32
+        )
     space_wait(1)
     owners_to_slab(1)
 
@@ -290,8 +316,7 @@
     bias_sum = jnp.zeros((TALL, 1), F32)
     for n in range(9):
         columns = slice(256 * n, 256 * n + 256)
-        pre = times(full, inv[n, 0], inv[n, 1])
-        pre = pre + jnp.dot(to_out, values[:, columns].astype(BF16), preferred_element_type=F32) + bias
+        pre = times(full, inv[n, 0], inv[n, 1]) + grads[:, columns]
         square = pre * pre
         bend = jnp.tanh(rate * (pre + 0.044715 * (square * pre)))
         half = 0.5 * (1.0 + bend)
@@ -299,9 +324,9 @@
         active = half * pre
         for p in range(PLANES):
             out_vmem[0, 0, p, :, columns] = active[ROWS * p : ROWS * p + C].astype(BF16)
-            grads[ROWS * p : ROWS * p + C, columns] = slope[ROWS * p : ROWS * p + C] * cot[0, 0, p, :, columns].astype(F32)
-            grads[ROWS * p + C : ROWS * p + ROWS, columns] = jnp.zeros((ROWS - C, 256), F32)
-        bias_sum = bias_sum + jnp.sum(grads[:, columns], axis=1, keepdims=True)
+        slope = slope * slopes[:, columns]
+        grads[:, columns] = slope
+        bias_sum = bias_sum + jnp.sum(slope, axis=1, keepdims=True)
     store_out = pltpu.make_async_copy(out_vmem, out_hbm, store_sem.at[0])
     store_out.start()
 
@@ -337,44 +362,51 @@
     along_x(grad_modes, row)
     gather_start(1, grad_modes, all_grads)
 
-    def grad_step(c, carry):
-        w_real, w_imag = weight[0, c].astype(F32), weight[1, c].astype(F32)
-        g_real, g_imag = grad_modes[0, :, :MODES], grad_modes[1, :, :MODES]
-        mixed[0, pl.ds(c, 1), :MODES] = jnp.sum(w_real * g_real + w_imag * g_imag, axis=0, keepdims=True)
-        mixed[1, pl.ds(c, 1), :MODES] = jnp.sum(w_real * g_imag - w_imag * g_real, axis=0, keepdims=True)
+    def grad_step(j, carry):
+        strip = strip_at(j)
+        slope = grad_modes[j]
+        crossed = other(slope)
+        for c in range(C):
+            weights = maps[c, :, strip]
+            mixed[j, 2 * c : 2 * c + 1, :] = jnp.sum(weights * slope, axis=0, keepdims=True)
+            mixed[j, 2 * c + 1 : 2 * c + 2, :] = jnp.sum(weights * crossed, axis=0, keepdims=True)
         return carry
 
-    lax.fori_loop(0, C, grad_step, 0)
+    lax.fori_loop(0, 4, grad_step, 0)
     back_along_x()
     planes_to_slabs(3, point)
     space_start(3)
 
+    partial8 = partial.reshape(8, 25, 4, 128)
+    gathered8 = gathered.reshape(4, 8, 25, 4, 128)
+    gathered_pairs = gathered.reshape(4, C, C, 2, 128)
     for r in range(1, 8):
         gather_copy(0, modes, all_modes, r).wait()
         gather_copy(1, grad_modes, all_grads, r).wait()
 
-    def part_step(c, carry):
-        total = jnp.zeros((C, 128), F32)
-        for b in range(8):
-            g_real, g_imag = all_grads[b, 0], all_grads[b, 1]
-            first = jnp.where(core == 0, g_real, g_imag)
-            second = jnp.where(core == 0, g_imag, -g_real)
-            total = total + all_modes[b, 0, pl.ds(c, 1), :] * first + all_modes[b, 1, pl.ds(c, 1), :] * second
-        partial[c] = total
-        return carry
-
-    lax.fori_loop(0, C, part_step, 0)
-
     def scatter_copy(r):
         to = (z_hi + r) % 4
         return pltpu.make_async_remote_copy(
-            src_ref=partial.at[pl.ds(to * 5, 5)], dst_ref=landed.at[r - 1],
+            src_ref=partial8.at[to * 2 + core], dst_ref=landed.at[r - 1],
             send_sem=dp_send.at[2, r], recv_sem=dp_recv.at[2, r],
             device_id=(to * 8 + eight, me), device_id_type=MESH,
         )
 
-    for r in range(1, 4):
-        scatter_copy(r).start()
+    for r in (2, 1, 3, 0):
+        start = (z_hi + r) % 4 * 5 + 2 * core
+
+        def part_step(i, carry):
+            first, second = jnp.zeros((PAIRS, 128), F32), jnp.zeros((PAIRS, 128), F32)
+            for b in range(8):
+                slope = all_grads[b]
+                first = first + all_modes[b, pl.ds(2 * (start + i), 1), :] * slope
+                second = second + all_modes[b, pl.ds(2 * (start + i) + 1, 1), :] * slope
+            partial[start + i] = first + other(second)
+            return carry
+
+        lax.fori_loop(0, 3, part_step, 0)
+        if r != 0:
+            scatter_copy(r).start()
 
     bias_total = jnp.zeros((C, 128), F32)
     for s in range(SLABS):
@@ -384,8 +416,7 @@
     point_total = jnp.zeros((C, 128), F32)
     for s in range(SLABS):
         point_total = point_total + recv[3, s]
-    small_sum = jnp.where(lane >= 108, point_total, jnp.where(lane == 0, turn(bias_total, 20), 0.0))
-    sums8[eight] = small_sum
+    sums8[eight] = jnp.where(lane >= 108, point_total, jnp.where(lane == 0, turn(bias_total, 20), 0.0))
 
     def eight_copy(r):
         to = (eight + r) % 8
@@ -397,25 +428,6 @@
 
     for r in range(1, 8):
         eight_copy(r).start()
-
-    for r in range(1, 4):
-        scatter_copy(r).wait()
-    for j in range(5):
-        gathered[x_pos, core, z_hi * 5 + j] = (
-            partial[z_hi * 5 + j] + landed[0, j] + landed[1, j] + landed[2, j]
-        )
-
-    def z_copy(r):
-        to = (z_hi + r) % 4
-        block = gathered.at[x_pos, core, pl.ds(z_hi * 5, 5)]
-        return pltpu.make_async_remote_copy(
-            src_ref=block, dst_ref=block,
-            send_sem=dp_send.at[4, r], recv_sem=dp_recv.at[4, r],
-            device_id=(to * 8 + eight, me), device_id_type=MESH,
-        )
-
-    for r in range(1, 4):
-        z_copy(r).start()
 
     full = lined[...]
     for n in range(9):
@@ -426,6 +438,47 @@
     store_grad = pltpu.make_async_copy(grad_vmem, grad_hbm, store_sem.at[1])
     store_grad.start()
 
+    for r in range(1, 4):
+        scatter_copy(r).wait()
+    gathered8[x_pos, z_hi * 2 + core] = partial8[z_hi * 2 + core] + landed[0] + landed[1] + landed[2]
+
+    def z_copy(r):
+        block = gathered8.at[x_pos, z_hi * 2 + core]
+        return pltpu.make_async_remote_copy(
+            src_ref=block, dst_ref=block,
+            send_sem=dp_send.at[4, r], recv_sem=dp_recv.at[4, r],
+            device_id=((z_hi + r) % 4 * 8 + eight, me), device_id_type=MESH,
+        )
+
+    def x_copy(k, r):
+        block = gathered8.at[x_pos, (z_hi - k) % 4 * 2 + core]
+        return pltpu.make_async_remote_copy(
+            src_ref=block, dst_ref=block,
+            send_sem=x_send.at[k, r], recv_sem=x_recv.at[k, r],
+            device_id=(z_hi * 8 + (x_pos + r) % 4 * 2 + core, me), device_id_type=MESH,
+        )
+
+    def core_copy(k):
+        block = gathered8.at[:, (z_hi - k) % 4 * 2 + core]
+        return pltpu.make_async_remote_copy(
+            src_ref=block, dst_ref=block,
+            send_sem=dp_send.at[6, k], recv_sem=dp_recv.at[6, k],
+            device_id=(z_hi * 8 + x_pos * 2 + 1 - core, me), device_id_type=MESH,
+        )
+
+    def spec_store(k, strip):
+        rows = pl.ds((z_hi - k) % 4 * 5, 5)
+        return pltpu.make_async_copy(
+            gathered_pairs.at[strip, rows],
+            spec_hbm.at[rows, :, :, 128 * strip : 128 * strip + 128],
+            spec_sem.at[k, strip],
+        )
+
+    for r in (2, 1, 3):
+        z_copy(r).start()
+    for r in (2, 1, 3):
+        x_copy(0, r).start()
+
     for r in range(1, 8):
         eight_copy(r).wait()
     total = sums8[0]
@@ -443,66 +496,41 @@
 
     for r in range(1, 4):
         four_copy(r).start()
-
-    for r in range(1, 4):
-        z_copy(r).wait()
-
-    def x_copy(r):
-        to = (x_pos + r) % 4
-        block = gathered.at[x_pos, core]
-        return pltpu.make_async_remote_copy(
-            src_ref=block, dst_ref=block,
-            send_sem=dp_send.at[6, r], recv_sem=dp_recv.at[6, r],
-            device_id=(z_hi * 8 + to * 2 + core, me), device_id_type=MESH,
-        )
-
-    def core_copy(r):
-        block = gathered.at[(x_pos - r) % 4, core]
-        return pltpu.make_async_remote_copy(
-            src_ref=block, dst_ref=block,
-            send_sem=dp_send.at[7, r], recv_sem=dp_recv.at[7, r],
-            device_id=(z_hi * 8 + x_pos * 2 + 1 - core, me), device_id_type=MESH,
-        )
-
-    def strip_store(r, part):
-        strip = (x_pos - r) % 4
-        return pltpu.make_async_copy(
-            gathered.at[strip, part],
-            spec_hbm.at[part, :, :, pl.ds(pl.multiple_of(strip * 128, 128), 128)],
-            store_sem.at[2 + 2 * r + (part != core).astype(jnp.int32)],
-        )
-
-    for r in range(1, 4):
-        x_copy(r).start()
-    core_copy(0).start()
-    strip_store(0, core).start()
-    for r in (1, 3, 2):
-        x_copy(r).wait_recv()
-        core_copy(r).start()
-        strip_store(r, core).start()
+    for k in (1, 3, 2):
+        z_copy(k).wait_recv()
+        for r in (2, 1, 3):
+            x_copy(k, r).start()
+    order = (0, 1, 3, 2)
+    for index, k in enumerate(order):
+        for r in range(1, 4):
+            x_copy(k, r).wait_recv()
+        core_copy(k).start()
+        if index > 0:
+            core_copy(order[index - 1]).wait_recv()
+            for strip in range(4):
+                spec_store(order[index - 1], strip).start()
     for r in range(1, 4):
         four_copy(r).wait()
     sums_ref[...] = sums4[0] + sums4[1] + sums4[2] + sums4[3]
-    for r in (0, 1, 3, 2):
-        core_copy(r).wait()
-        strip_store(r, 1 - core).start()
+    core_copy(2).wait_recv()
+    for strip in range(4):
+        spec_store(2, strip).start()
     for r in range(1, 4):
-        x_copy(r).wait_send()
-    for r in range(4):
-        strip_store(r, core).wait()
-        strip_store(r, 1 - core).wait()
+        z_copy(r).wait_send()
+        for k in range(4):
+            x_copy(k, r).wait_send()
+    for k in order:
+        core_copy(k).wait_send()
+    for k in order:
+        for strip in range(4):
+            spec_store(k, strip).wait()
     store_out.wait()
     store_grad.wait()
 
 
 def on_device(wake_field, spec_weight, point_weight, bias_term, cotangent):
     forward, inverse, x_two, x_inverse, kz_weight = tables()
-    matrix = point_weight.astype(F32)
-    small = jnp.stack([
-        jnp.pad(matrix.T, ((0, ROWS - C), (0, 128 - C))),
-        jnp.pad(matrix, ((0, ROWS - C), (0, 128 - C))),
-        jnp.pad(jnp.broadcast_to(bias_term[:, None], (C, 128)), ((0, ROWS - C), (0, 0))),
-    ])
+    weight = spec_weight.transpose(1, 2, 0, 3)
     anywhere = pl.BlockSpec(memory_space=pl.ANY)
     inside = pl.BlockSpec(memory_space=pltpu.VMEM)
     field = wake_field.shape
@@ -511,54 +539,60 @@
         out_shape=(
             jax.ShapeDtypeStruct(field, BF16),
             jax.ShapeDtypeStruct(field, BF16),
-            jax.ShapeDtypeStruct((2, C, C, 512), F32),
+            jax.ShapeDtypeStruct((C, C, 2, 512), F32),
             jax.ShapeDtypeStruct((C, 128), F32),
         ),
-        in_specs=[anywhere, anywhere, anywhere, inside, inside, anywhere, anywhere, anywhere, anywhere],
+        in_specs=[anywhere] * 3 + [inside] * 3 + [anywhere] * 4,
         out_specs=(anywhere, anywhere, anywhere, inside),
         scratch_shapes=[
             pltpu.VMEM(field, BF16),
             pltpu.VMEM(field, BF16),
-            pltpu.VMEM(spec_weight.shape, BF16),
+            pltpu.VMEM(weight.shape, BF16),
             pltpu.VMEM(forward.shape, BF16),
             pltpu.VMEM(inverse.shape, BF16),
             pltpu.VMEM(x_two.shape, BF16),
             pltpu.VMEM(x_inverse.shape, BF16),
             pltpu.VMEM((TALL, CELLS), F32),
+            pltpu.VMEM((TALL, CELLS), F32),
+            pltpu.VMEM((C, PAIRS, 512), F32),
             pltpu.VMEM((TALL, WIDE), F32),
             pltpu.VMEM((TALL, WIDE), F32),
             pltpu.VMEM((TALL, CELLS), F32),
             pltpu.VMEM((TALL, WIDE), F32),
             pltpu.VMEM((TALL, 512), F32),
-            pltpu.VMEM((2, C, 512), F32),
-            pltpu.VMEM((2, C, 512), F32),
-            pltpu.VMEM((2, C, 512), F32),
+            pltpu.VMEM((4, PAIRS, 128), F32),
+            pltpu.VMEM((4, PAIRS, 128), F32),
+            pltpu.VMEM((4, PAIRS, 128), F32),
+            pltpu.VMEM((ROWS, 128), F32),
             pltpu.VMEM((4, SLABS, C, 128), F32),
             pltpu.VMEM((4, SLABS, C, 128), F32),
-            pltpu.VMEM((8, 2, C, 128), F32),
-            pltpu.VMEM((8, 2, C, 128), F32),
-            pltpu.VMEM((C, C, 128), F32),
-            pltpu.VMEM((3, 5, C, 128), F32),
-            pltpu.VMEM((4, 2, C, C, 128), F32),
+            pltpu.VMEM((8, PAIRS, 128), F32),
+            pltpu.VMEM((8, PAIRS, 128), F32),
+            pltpu.VMEM((C, PAIRS, 128), F32),
+            pltpu.VMEM((3, 25, 4, 128), F32),
+            pltpu.VMEM((4, C, PAIRS, 128), F32),
             pltpu.VMEM((8, C, 128), F32),
             pltpu.VMEM((4, C, 128), F32),
             pltpu.VMEM(field, BF16),
             pltpu.VMEM(field, BF16),
             pltpu.SemaphoreType.DMA((9,)),
-            pltpu.SemaphoreType.DMA((10,)),
+            pltpu.SemaphoreType.DMA((2,)),
+            pltpu.SemaphoreType.DMA((4, 4)),
             pltpu.SemaphoreType.DMA((4, 16)),
             pltpu.SemaphoreType.DMA((4, 16)),
-            pltpu.SemaphoreType.DMA((8, 8)),
-            pltpu.SemaphoreType.DMA((8, 8)),
+            pltpu.SemaphoreType.DMA((7, 8)),
+            pltpu.SemaphoreType.DMA((7, 8)),
+            pltpu.SemaphoreType.DMA((4, 4)),
+            pltpu.SemaphoreType.DMA((4, 4)),
         ],
         compiler_params=pltpu.CompilerParams(
             collective_id=0, has_side_effects=True, vmem_limit_bytes=56 * 1024 * 1024
         ),
-    )(wake_field, cotangent, spec_weight, small, kz_weight, forward, inverse, x_two, x_inverse)
+    )(wake_field, cotangent, weight, point_weight, bias_term[None], kz_weight, forward, inverse, x_two, x_inverse)
     return (
         output_field,
         grad_field,
-        grad_spec[..., :MODES],
+        grad_spec.transpose(2, 0, 1, 3)[..., :MODES],
         sums[:, 108:128],
         sums[:, 0],
     )

time: 90.7 us -> 84 us (0.926)
  Pallas kernels: 78.5 us -> 73.6 us
  other arithmetic: 1.34 us -> 0 us
    pallas_call x1, Pallas kernels: 78.5 us -> 73.6 us  [on_device(): pl.pallas_call(kernel, out_shape=(jax.ShapeDtypeStruct(field, BF16), jax....]
    unnamed x10 -> x3, local copies, waits for them, and re-layouts: 7.75 us -> 6.6 us
where the time goes in v1:
time: 84 us; the launch traced here: 83.6 us
  Pallas kernels  73.6 us (88%)
  local copies, waits for them, and re-layouts  9.31 us (11%)
    pallas_call x1, Pallas kernels, on_device(): pl.pallas_call(kernel, out_shape=(jax.ShapeDtypeStruct(field, BF16), jax....  73.6 us
    unnamed x3, local copies, waits for them, and re-layouts  6.6 us

profile of v1, /device:TPU:1, one launch (start us, length us, event | category | flops | bytes accessed | tf_op | source)
XLA Modules:
  0.0 83.6 jit_solution(14159028206187872295)
XLA Ops:
  0.6 73.6 %shard_map.137 = (bf16[1,1,3,20,2304]{4,3,2,1,0:T(8,128)(2,1)}, bf16[1,1,3,20,2304]{4,3,2,1,0:T(8,128)(2,1)}, f32[20,20,2,512]{3,2,1,0:T(2,128)}, f32[20,128]{1,0:T(8,128)}) custom-call(bf16[1,1,3,20,2304]{4,3,2,1,0:T(8,128)(2,1)} %wake_hbm.1, bf16[1,1,3,20,2304]{4,3,2,1,0:T(8,128)(2,1)} %cot_hbm.1, bf16[20,20,2,432]{3,2,1,0:T(2,128)(2,1)} %bitcast.5, ...), custom_call_target="tpu_custom_call" | custom-call | tf_op jit(solution)/shard_map/pallas_call | solution.py:537
  74.3 1.4 %slice.10 = f32[20,20]{1,0:T(8,128)} slice(f32[20,128]{1,0:T(8,128)} %get-tuple-element.12), slice={[0:20], [108:128]} | slice | bytes 3200 | tf_op jit(solution)/shard_map/slice | solution.py:596
  75.7 1.3 %slice_reduce_fusion = f32[20]{0:T(128)} fusion(f32[20,128]{1,0:T(8,128)} %get-tuple-element.12), kind=kLoop, calls=%fused_computation | loop fusion | bytes 160 | tf_op jit(solution)/shard_map/slice | solution.py:597
  77.0 1.7 %copy.18 = bf16[1,1,3,20,2304]{4,3,2,1,0:T(8,128)(2,1)} copy(bf16[1,1,3,20,2304]{4,3,2,1,0:T(8,128)(2,1)} %get-tuple-element.18) | data formatting | bytes 552960
  78.7 1.7 %copy.19 = bf16[1,1,3,20,2304]{4,3,2,1,0:T(8,128)(2,1)} copy(bf16[1,1,3,20,2304]{4,3,2,1,0:T(8,128)(2,1)} %get-tuple-element.19) | data formatting | bytes 552960
  80.4 3.2 %copy.20 = f32[2,20,20,432]{3,0,2,1:T(2,128)} copy(f32[2,20,20,432]{3,0,2,1:T(2,128)} %bitcast.4) | data formatting | bytes 2764800

commit v2 on v1

--- a/solution.py
+++ b/solution.py
@@ -27,6 +27,7 @@
 TILES = 6
 WIDE = TILES * 128
 PAIRS = 2 * C
+SPLIT = 19
 
 
 def wave(i):
@@ -101,7 +102,7 @@
     values, slopes, maps, spectra, slab, grads, lined, pieces, modes, mixed, grad_modes, matrix,
     send, recv, all_modes, all_grads, partial, landed, gathered, sums8, sums4,
     out_vmem, grad_vmem,
-    load_sem, store_sem, spec_sem, send_sem, recv_sem, dp_send, dp_recv, x_send, x_recv,
+    load_sem, store_sem, spec_sem, send_sem, recv_sem, dp_send, dp_recv, x_send, x_recv, z_send, z_recv,
 ):
     dp = lax.axis_index("dp")
     me = lax.axis_index("space")
@@ -442,21 +443,32 @@
         scatter_copy(r).wait()
     gathered8[x_pos, z_hi * 2 + core] = partial8[z_hi * 2 + core] + landed[0] + landed[1] + landed[2]
 
+    def own(k):
+        return (z_hi - k) % 4 * 2 + core
+
+    def to_z(block, send_at, recv_at, r):
+        return pltpu.make_async_remote_copy(
+            src_ref=block, dst_ref=block, send_sem=send_at, recv_sem=recv_at,
+            device_id=((z_hi + r) % 4 * 8 + eight, me), device_id_type=MESH,
+        )
+
+    def to_x(block, send_at, recv_at, r):
+        return pltpu.make_async_remote_copy(
+            src_ref=block, dst_ref=block, send_sem=send_at, recv_sem=recv_at,
+            device_id=(z_hi * 8 + (x_pos + r) % 4 * 2 + core, me), device_id_type=MESH,
+        )
+
     def z_copy(r):
-        block = gathered8.at[x_pos, z_hi * 2 + core]
-        return pltpu.make_async_remote_copy(
-            src_ref=block, dst_ref=block,
-            send_sem=dp_send.at[4, r], recv_sem=dp_recv.at[4, r],
-            device_id=((z_hi + r) % 4 * 8 + eight, me), device_id_type=MESH,
-        )
+        return to_z(gathered8.at[x_pos, own(0), 0:SPLIT], dp_send.at[4, r], dp_recv.at[4, r], r)
 
     def x_copy(k, r):
-        block = gathered8.at[x_pos, (z_hi - k) % 4 * 2 + core]
-        return pltpu.make_async_remote_copy(
-            src_ref=block, dst_ref=block,
-            send_sem=x_send.at[k, r], recv_sem=x_recv.at[k, r],
-            device_id=(z_hi * 8 + (x_pos + r) % 4 * 2 + core, me), device_id_type=MESH,
-        )
+        return to_x(gathered8.at[x_pos, own(k), 0:SPLIT], x_send.at[k, r], x_recv.at[k, r], r)
+
+    def x_first(r):
+        return to_x(gathered8.at[x_pos, own(0), SPLIT:25], dp_send.at[7, r], dp_recv.at[7, r], r)
+
+    def z_second(j, r):
+        return to_z(gathered8.at[(x_pos - j) % 4, own(0), SPLIT:25], z_send.at[j, r], z_recv.at[j, r], r)
 
     def core_copy(k):
         block = gathered8.at[:, (z_hi - k) % 4 * 2 + core]
@@ -475,8 +487,11 @@
         )
 
     for r in (2, 1, 3):
+        x_first(r).start()
+    for r in (2, 1, 3):
         z_copy(r).start()
     for r in (2, 1, 3):
+        z_second(0, r).start()
         x_copy(0, r).start()
 
     for r in range(1, 8):
@@ -496,6 +511,10 @@
 
     for r in range(1, 4):
         four_copy(r).start()
+    for j in (1, 3, 2):
+        x_first(j).wait_recv()
+        for r in (2, 1, 3):
+            z_second(j, r).start()
     for k in (1, 3, 2):
         z_copy(k).wait_recv()
         for r in (2, 1, 3):
@@ -504,6 +523,9 @@
     for index, k in enumerate(order):
         for r in range(1, 4):
             x_copy(k, r).wait_recv()
+        if k != 0:
+            for j in range(4):
+                z_second(j, k).wait_recv()
         core_copy(k).start()
         if index > 0:
             core_copy(order[index - 1]).wait_recv()
@@ -511,12 +533,18 @@
                 spec_store(order[index - 1], strip).start()
     for r in range(1, 4):
         four_copy(r).wait()
-    sums_ref[...] = sums4[0] + sums4[1] + sums4[2] + sums4[3]
+    total = turn(sums4[0] + sums4[1] + sums4[2] + sums4[3], 20)
+    sums_ref[0:C, :] = total
+    square = lax.broadcasted_iota(jnp.int32, (C, 128), 0) == lane
+    sums_ref[C : C + 1, :] = jnp.sum(jnp.where(square, total[:, C : C + 1], 0.0), axis=0, keepdims=True)
     core_copy(2).wait_recv()
     for strip in range(4):
         spec_store(2, strip).start()
     for r in range(1, 4):
         z_copy(r).wait_send()
+        x_first(r).wait_send()
+        for j in range(4):
+            z_second(j, r).wait_send()
         for k in range(4):
             x_copy(k, r).wait_send()
     for k in order:
@@ -526,6 +554,22 @@
             spec_store(k, strip).wait()
     store_out.wait()
     store_grad.wait()
+
+
+def results(out_from, grad_from, spec_from, sums, out_to, grad_to, spec_to, point_to, bias_to, sem):
+    copies = []
+    for j in range(10):
+        rows = pl.ds(2 * j, 2)
+        copies.append(pltpu.make_async_copy(spec_from.at[rows], spec_to.at[rows], sem.at[j]))
+    for p in range(PLANES):
+        copies.append(pltpu.make_async_copy(out_from.at[0, 0, p], out_to.at[0, 0, p], sem.at[10 + p]))
+        copies.append(pltpu.make_async_copy(grad_from.at[0, 0, p], grad_to.at[0, 0, p], sem.at[13 + p]))
+    for copy in copies:
+        copy.start()
+    point_to[...] = sums[0:C, 0:C]
+    bias_to[...] = sums[C : C + 1, 0:C]
+    for copy in copies:
+        copy.wait()
 
 
 def on_device(wake_field, spec_weight, point_weight, bias_term, cotangent):
@@ -540,7 +584,7 @@
             jax.ShapeDtypeStruct(field, BF16),
             jax.ShapeDtypeStruct(field, BF16),
             jax.ShapeDtypeStruct((C, C, 2, 512), F32),
-            jax.ShapeDtypeStruct((C, 128), F32),
+            jax.ShapeDtypeStruct((ROWS, 128), F32),
         ),
         in_specs=[anywhere] * 3 + [inside] * 3 + [anywhere] * 4,
         out_specs=(anywhere, anywhere, anywhere, inside),
@@ -580,8 +624,10 @@
             pltpu.SemaphoreType.DMA((4, 4)),
             pltpu.SemaphoreType.DMA((4, 16)),
             pltpu.SemaphoreType.DMA((4, 16)),
-            pltpu.SemaphoreType.DMA((7, 8)),
-            pltpu.SemaphoreType.DMA((7, 8)),
+            pltpu.SemaphoreType.DMA((8, 8)),
+            pltpu.SemaphoreType.DMA((8, 8)),
+            pltpu.SemaphoreType.DMA((4, 4)),
+            pltpu.SemaphoreType.DMA((4, 4)),
             pltpu.SemaphoreType.DMA((4, 4)),
             pltpu.SemaphoreType.DMA((4, 4)),
         ],
@@ -589,12 +635,25 @@
             collective_id=0, has_side_effects=True, vmem_limit_bytes=56 * 1024 * 1024
         ),
     )(wake_field, cotangent, weight, point_weight, bias_term[None], kz_weight, forward, inverse, x_two, x_inverse)
+    output_field, grad_field, grad_spec, grad_point, grad_bias = pl.pallas_call(
+        results,
+        out_shape=(
+            jax.ShapeDtypeStruct(field, BF16),
+            jax.ShapeDtypeStruct(field, BF16),
+            jax.ShapeDtypeStruct((C, C, 2, 512), F32),
+            jax.ShapeDtypeStruct((C, C), F32),
+            jax.ShapeDtypeStruct((1, C), F32),
+        ),
+        in_specs=[anywhere] * 3 + [inside],
+        out_specs=(anywhere, anywhere, anywhere, inside, inside),
+        scratch_shapes=[pltpu.SemaphoreType.DMA((16,))],
+    )(output_field, grad_field, grad_spec, sums)
     return (
         output_field,
         grad_field,
         grad_spec.transpose(2, 0, 1, 3)[..., :MODES],
-        sums[:, 108:128],
-        sums[:, 0],
+        grad_point,
+        grad_bias.reshape(C),
     )
 
 

time: 84 us -> 145 us (1.73)
  Pallas kernels: 73.6 us -> 144 us
  local copies, waits for them, and re-layouts: 9.31 us -> 0 us
    pallas_call x0 -> x1, Pallas kernels: none -> 72.3 us  [on_device(): pl.pallas_call(results, out_shape=(jax.ShapeDtypeStruct(field, BF16), jax...]
    unnamed x3 -> x0, local copies, waits for them, and re-layouts: 6.6 us -> none
    slice x2 -> x0, local copies, waits for them, and re-layouts: 2.71 us -> none  [the longest x1 1.38 us: on_device(): sums[:, 108:128]]
where the time goes in v2:
time: 145 us
  Pallas kernels  144 us (99%)
    pallas_call x1, Pallas kernels, on_device(): pl.pallas_call(results, out_shape=(jax.ShapeDtypeStruct(field, BF16), jax...  72.3 us
    pallas_call x1, Pallas kernels, on_device(): pl.pallas_call(kernel, out_shape=(jax.ShapeDtypeStruct(field, BF16), jax....  72.2 us

profile of v2, /device:TPU:1, one launch (start us, length us, event | category | flops | bytes accessed | tf_op | source)
XLA Modules:
  0.0 145.1 jit_solution(13646233669736858407)
XLA Ops:
  0.6 72.2 %shard_map.137 = (bf16[1,1,3,20,2304]{4,3,2,1,0:T(8,128)(2,1)}, bf16[1,1,3,20,2304]{4,3,2,1,0:T(8,128)(2,1)}, f32[20,20,2,512]{3,2,1,0:T(2,128)}, f32[24,128]{1,0:T(8,128)}) custom-call(bf16[1,1,3,20,2304]{4,3,2,1,0:T(8,128)(2,1)} %wake_hbm.1, bf16[1,1,3,20,2304]{4,3,2,1,0:T(8,128)(2,1)} %cot_hbm.1, bf16[20,20,2,432]{3,2,1,0:T(2,128)(2,1)} %bitcast.5, ...), custom_call_target="tpu_custom_call" | custom-call | tf_op jit(solution)/shard_map/pallas_call | solution.py:581
  72.8 72.3 %shard_map.138 = (bf16[1,1,3,20,2304]{4,3,2,1,0:T(8,128)(2,1)}, bf16[1,1,3,20,2304]{4,3,2,1,0:T(8,128)(2,1)}, f32[20,20,2,512]{3,2,1,0:T(2,128)}, f32[20,20]{1,0:T(8,128)}, f32[1,20]{1,0:T(1,128)}) custom-call(bf16[1,1,3,20,2304]{4,3,2,1,0:T(8,128)(2,1)} %get-tuple-element.14.out_from, bf16[1,1,3,20,2304]{4,3,2,1,0:T(8,128)(2,1)} %get-tuple-element.15.grad_from, ...), custom_call_target="tpu_custom_call" | custom-call | tf_op jit(solution)/shard_map/pallas_call | solution.py:638

commit v3 on v2

--- a/solution.py
+++ b/solution.py
@@ -97,12 +97,11 @@
 
 def kernel(
     wake_hbm, cot_hbm, weight_hbm, point_weight, bias_term, kz_weight, fwd_hbm, inv_hbm, x_hbm, xt_hbm,
-    out_hbm, grad_hbm, spec_hbm, sums_ref,
+    out_vmem, grad_vmem, gathered, sums_ref,
     wake, cot, weight, fwd, inv, xf, xt,
     values, slopes, maps, spectra, slab, grads, lined, pieces, modes, mixed, grad_modes, matrix,
-    send, recv, all_modes, all_grads, partial, landed, gathered, sums8, sums4,
-    out_vmem, grad_vmem,
-    load_sem, store_sem, spec_sem, send_sem, recv_sem, dp_send, dp_recv, x_send, x_recv, z_send, z_recv,
+    send, recv, all_modes, all_grads, partial, landed, sums8, sums4,
+    load_sem, send_sem, recv_sem, dp_send, dp_recv, x_send, x_recv, z_send, z_recv,
 ):
     dp = lax.axis_index("dp")
     me = lax.axis_index("space")
@@ -328,8 +327,6 @@
         slope = slope * slopes[:, columns]
         grads[:, columns] = slope
         bias_sum = bias_sum + jnp.sum(slope, axis=1, keepdims=True)
-    store_out = pltpu.make_async_copy(out_vmem, out_hbm, store_sem.at[0])
-    store_out.start()
 
     full = grads[...]
     for n in range(3):
@@ -380,7 +377,6 @@
 
     partial8 = partial.reshape(8, 25, 4, 128)
     gathered8 = gathered.reshape(4, 8, 25, 4, 128)
-    gathered_pairs = gathered.reshape(4, C, C, 2, 128)
     for r in range(1, 8):
         gather_copy(0, modes, all_modes, r).wait()
         gather_copy(1, grad_modes, all_grads, r).wait()
@@ -436,8 +432,6 @@
         result = times(full, inv[n, 0], inv[n, 1]) + values[:, columns]
         for p in range(PLANES):
             grad_vmem[0, 0, p, :, columns] = result[ROWS * p : ROWS * p + C].astype(BF16)
-    store_grad = pltpu.make_async_copy(grad_vmem, grad_hbm, store_sem.at[1])
-    store_grad.start()
 
     for r in range(1, 4):
         scatter_copy(r).wait()
@@ -476,14 +470,6 @@
             src_ref=block, dst_ref=block,
             send_sem=dp_send.at[6, k], recv_sem=dp_recv.at[6, k],
             device_id=(z_hi * 8 + x_pos * 2 + 1 - core, me), device_id_type=MESH,
-        )
-
-    def spec_store(k, strip):
-        rows = pl.ds((z_hi - k) % 4 * 5, 5)
-        return pltpu.make_async_copy(
-            gathered_pairs.at[strip, rows],
-            spec_hbm.at[rows, :, :, 128 * strip : 128 * strip + 128],
-            spec_sem.at[k, strip],
         )
 
     for r in (2, 1, 3):
@@ -520,26 +506,19 @@
         for r in (2, 1, 3):
             x_copy(k, r).start()
     order = (0, 1, 3, 2)
-    for index, k in enumerate(order):
+    for k in order:
         for r in range(1, 4):
             x_copy(k, r).wait_recv()
         if k != 0:
             for j in range(4):
                 z_second(j, k).wait_recv()
         core_copy(k).start()
-        if index > 0:
-            core_copy(order[index - 1]).wait_recv()
-            for strip in range(4):
-                spec_store(order[index - 1], strip).start()
     for r in range(1, 4):
         four_copy(r).wait()
     total = turn(sums4[0] + sums4[1] + sums4[2] + sums4[3], 20)
     sums_ref[0:C, :] = total
     square = lax.broadcasted_iota(jnp.int32, (C, 128), 0) == lane
     sums_ref[C : C + 1, :] = jnp.sum(jnp.where(square, total[:, C : C + 1], 0.0), axis=0, keepdims=True)
-    core_copy(2).wait_recv()
-    for strip in range(4):
-        spec_store(2, strip).start()
     for r in range(1, 4):
         z_copy(r).wait_send()
         x_first(r).wait_send()
@@ -548,22 +527,23 @@
         for k in range(4):
             x_copy(k, r).wait_send()
     for k in order:
-        core_copy(k).wait_send()
-    for k in order:
-        for strip in range(4):
-            spec_store(k, strip).wait()
-    store_out.wait()
-    store_grad.wait()
+        core_copy(k).wait()
 
 
 def results(out_from, grad_from, spec_from, sums, out_to, grad_to, spec_to, point_to, bias_to, sem):
     copies = []
-    for j in range(10):
-        rows = pl.ds(2 * j, 2)
-        copies.append(pltpu.make_async_copy(spec_from.at[rows], spec_to.at[rows], sem.at[j]))
+    strips = spec_from.reshape(4, C, C, 2, 128)
+    for j in range(4):
+        for k in range(4):
+            rows = pl.ds(5 * k, 5)
+            copies.append(
+                pltpu.make_async_copy(
+                    strips.at[j, rows], spec_to.at[rows, :, :, 128 * j : 128 * j + 128], sem.at[4 * j + k]
+                )
+            )
     for p in range(PLANES):
-        copies.append(pltpu.make_async_copy(out_from.at[0, 0, p], out_to.at[0, 0, p], sem.at[10 + p]))
-        copies.append(pltpu.make_async_copy(grad_from.at[0, 0, p], grad_to.at[0, 0, p], sem.at[13 + p]))
+        copies.append(pltpu.make_async_copy(out_from.at[0, 0, p], out_to.at[0, 0, p], sem.at[16 + p]))
+        copies.append(pltpu.make_async_copy(grad_from.at[0, 0, p], grad_to.at[0, 0, p], sem.at[19 + p]))
     for copy in copies:
         copy.start()
     point_to[...] = sums[0:C, 0:C]
@@ -581,13 +561,13 @@
     output_field, grad_field, grad_spec, sums = pl.pallas_call(
         kernel,
         out_shape=(
-            jax.ShapeDtypeStruct(field, BF16),
-            jax.ShapeDtypeStruct(field, BF16),
-            jax.ShapeDtypeStruct((C, C, 2, 512), F32),
-            jax.ShapeDtypeStruct((ROWS, 128), F32),
+            pltpu.VMEM(field, BF16),
+            pltpu.VMEM(field, BF16),
+            pltpu.VMEM((4, C, PAIRS, 128), F32),
+            pltpu.VMEM((ROWS, 128), F32),
         ),
         in_specs=[anywhere] * 3 + [inside] * 3 + [anywhere] * 4,
-        out_specs=(anywhere, anywhere, anywhere, inside),
+        out_specs=(inside, inside, inside, inside),
         scratch_shapes=[
             pltpu.VMEM(field, BF16),
             pltpu.VMEM(field, BF16),
@@ -614,14 +594,9 @@
             pltpu.VMEM((8, PAIRS, 128), F32),
             pltpu.VMEM((C, PAIRS, 128), F32),
             pltpu.VMEM((3, 25, 4, 128), F32),
-            pltpu.VMEM((4, C, PAIRS, 128), F32),
             pltpu.VMEM((8, C, 128), F32),
             pltpu.VMEM((4, C, 128), F32),
-            pltpu.VMEM(field, BF16),
-            pltpu.VMEM(field, BF16),
             pltpu.SemaphoreType.DMA((9,)),
-            pltpu.SemaphoreType.DMA((2,)),
-            pltpu.SemaphoreType.DMA((4, 4)),
             pltpu.SemaphoreType.DMA((4, 16)),
             pltpu.SemaphoreType.DMA((4, 16)),
             pltpu.SemaphoreType.DMA((8, 8)),
@@ -632,7 +607,7 @@
             pltpu.SemaphoreType.DMA((4, 4)),
         ],
         compiler_params=pltpu.CompilerParams(
-            collective_id=0, has_side_effects=True, vmem_limit_bytes=56 * 1024 * 1024
+            collective_id=0, has_side_effects=True, vmem_limit_bytes=52 * 1024 * 1024
         ),
     )(wake_field, cotangent, weight, point_weight, bias_term[None], kz_weight, forward, inverse, x_two, x_inverse)
     output_field, grad_field, grad_spec, grad_point, grad_bias = pl.pallas_call(
@@ -644,10 +619,10 @@
             jax.ShapeDtypeStruct((C, C), F32),
             jax.ShapeDtypeStruct((1, C), F32),
         ),
-        in_specs=[anywhere] * 3 + [inside],
+        in_specs=[inside] * 4,
         out_specs=(anywhere, anywhere, anywhere, inside, inside),
-        scratch_shapes=[pltpu.SemaphoreType.DMA((16,))],
-    )(output_field, grad_field, grad_spec, sums)
+        scratch_shapes=[pltpu.SemaphoreType.DMA((22,))],
+    )(*[pltpu.with_memory_space_constraint(array, pltpu.VMEM) for array in (output_field, grad_field, grad_spec, sums)])
     return (
         output_field,
         grad_field,

time: 145 us -> 73.7 us (0.51)
  Pallas kernels: 144 us -> 72.7 us
    pallas_call x1, Pallas kernels: 72.3 us -> 2.17 us  [on_device(): pl.pallas_call(results, out_shape=(jax.ShapeDtypeStruct(field, BF16), jax...]
    pallas_call x1, Pallas kernels: 72.2 us -> 70.6 us  [on_device(): pl.pallas_call(kernel, out_shape=(pltpu.VMEM(field, BF16), pltpu.VMEM(fie...]
where the time goes in v3:
time: 73.7 us; the launch traced here: 73.4 us
  Pallas kernels  72.7 us (99%)
    pallas_call x1, Pallas kernels, on_device(): pl.pallas_call(kernel, out_shape=(pltpu.VMEM(field, BF16), pltpu.VMEM(fie...  70.6 us
    pallas_call x1, Pallas kernels, on_device(): pl.pallas_call(results, out_shape=(jax.ShapeDtypeStruct(field, BF16), jax...  2.17 us

profile of v3, /device:TPU:1, one launch (start us, length us, event | category | flops | bytes accessed | tf_op | source)
XLA Modules:
  0.0 73.4 jit_solution(7055470227073747938)
XLA Ops:
  0.6 70.6 %shard_map.137 = (bf16[1,1,3,20,2304]{4,3,2,1,0:T(8,128)(2,1)S(1)}, bf16[1,1,3,20,2304]{4,3,2,1,0:T(8,128)(2,1)S(1)}, f32[4,20,40,128]{3,2,1,0:T(8,128)S(1)}, f32[24,128]{1,0:T(8,128)S(1)}) custom-call(bf16[1,1,3,20,2304]{4,3,2,1,0:T(8,128)(2,1)} %wake_hbm.1, bf16[1,1,3,20,2304]{4,3,2,1,0:T(8,128)(2,1)} %cot_hbm.1, bf16[20,20,2,432]{3,2,1,0:T(2,128)(2,1)} %bitcast.5, ...), custom_call_target="tpu_custom_call" | custom-call | tf_op jit(solution)/shard_map/pallas_call | solution.py:561
  71.2 2.2 %shard_map.138 = (bf16[1,1,3,20,2304]{4,3,2,1,0:T(8,128)(2,1)}, bf16[1,1,3,20,2304]{4,3,2,1,0:T(8,128)(2,1)}, f32[20,20,2,512]{3,2,1,0:T(2,128)}, f32[20,20]{1,0:T(8,128)}, f32[1,20]{1,0:T(1,128)}) custom-call(bf16[1,1,3,20,2304]{4,3,2,1,0:T(8,128)(2,1)S(1)} %get-tuple-element.14.out_from, bf16[1,1,3,20,2304]{4,3,2,1,0:T(8,128)(2,1)S(1)} %get-tuple-element.15.grad_from, ...), custom_call_target="tpu_custom_call" | custom-call | tf_op jit(solution)/shard_map/pallas_call | solution.py:613

commit v4 on v3

--- a/solution.py
+++ b/solution.py
@@ -27,7 +27,7 @@
 TILES = 6
 WIDE = TILES * 128
 PAIRS = 2 * C
-SPLIT = 19
+SPLIT = 8
 
 
 def wave(i):
@@ -100,8 +100,8 @@
     out_vmem, grad_vmem, gathered, sums_ref,
     wake, cot, weight, fwd, inv, xf, xt,
     values, slopes, maps, spectra, slab, grads, lined, pieces, modes, mixed, grad_modes, matrix,
-    send, recv, all_modes, all_grads, partial, landed, sums8, sums4,
-    load_sem, send_sem, recv_sem, dp_send, dp_recv, x_send, x_recv, z_send, z_recv,
+    send, recv, all_modes, all_grads, partial, landed, own_sum, sums8, sums4,
+    load_sem, local_sem, send_sem, recv_sem, dp_send, dp_recv, x_send, x_recv, z_send, z_recv,
 ):
     dp = lax.axis_index("dp")
     me = lax.axis_index("space")
@@ -110,7 +110,8 @@
     lane = lax.broadcasted_iota(jnp.int32, (C, 128), 1)
     third = lane // 36
     slot = jnp.where(lane < 108, lane % 36 // 12, 3)
-    even = lax.broadcasted_iota(jnp.int32, (PAIRS, 128), 0) % 2 == 0
+    home = z_hi * 4 + x_pos
+    far_first = (8, 7, 9, 6, 10, 5, 11, 4, 12, 3, 13, 2, 14, 1, 15)
 
     loads = [
         pltpu.make_async_copy(wake_hbm, wake, load_sem.at[0]),
@@ -132,9 +133,10 @@
     for r in range(1, 8):
         peer = z_hi * 8 + (eight + r) % 8
         pl.semaphore_signal(barrier, inc=1, device_id=(peer, me), device_id_type=MESH)
-    for r in range(1, 4):
-        peer = (z_hi + r) % 4 * 8 + eight
-        pl.semaphore_signal(barrier, inc=1, device_id=(peer, me), device_id_type=MESH)
+    for i in range(1, 4):
+        for j in range(4):
+            peer = (z_hi + i) % 4 * 8 + (x_pos + j) % 4 * 2 + core
+            pl.semaphore_signal(barrier, inc=1, device_id=(peer, me), device_id_type=MESH)
 
     values[...] = jnp.zeros((TALL, CELLS), F32)
     lined[...] = jnp.zeros((TALL, WIDE), F32)
@@ -164,7 +166,9 @@
         return value if shift == 0 else pltpu.roll(value, shift, 1)
 
     def other(value):
-        return jnp.where(even, pltpu.roll(value, PAIRS - 1, 0), -pltpu.roll(value, 1, 0))
+        rows = value.shape[0]
+        even = lax.broadcasted_iota(jnp.int32, (rows, 128), 0) % 2 == 0
+        return jnp.where(even, pltpu.roll(value, rows - 1, 0), -pltpu.roll(value, 1, 0))
 
     def choose(where, parts):
         total = jnp.zeros((C, 128), F32)
@@ -235,18 +239,32 @@
     def strip_at(index):
         return pl.ds(pl.multiple_of(index * 128, 128), 128)
 
-    def gather_copy(kind, source, target, r):
-        to = (eight + r) % 8
-        return pltpu.make_async_remote_copy(
-            src_ref=source.at[to // 2], dst_ref=target.at[eight],
-            send_sem=dp_send.at[kind, r], recv_sem=dp_recv.at[kind, r],
-            device_id=(z_hi * 8 + to, me), device_id_type=MESH,
-        )
-
-    def gather_start(kind, source, target):
-        for r in range(1, 8):
-            gather_copy(kind, source, target, r).start()
-        target[eight] = source[x_pos]
+    grad_pairs = grad_modes.reshape(4, C, 2, 128)
+    landing = all_grads.reshape(16, 8, 2, 128)
+
+    def gather_to(r):
+        to = (home + r) % 16
+        return to // 4, to % 4, (to * 2 + core, me)
+
+    def modes_copy(r):
+        _, x_to, device = gather_to(r)
+        return pltpu.make_async_remote_copy(
+            src_ref=modes.at[x_to], dst_ref=all_modes.at[home],
+            send_sem=dp_send.at[0, r], recv_sem=dp_recv.at[0, r],
+            device_id=device, device_id_type=MESH,
+        )
+
+    def grads_copy(r):
+        z_to, x_to, device = gather_to(r)
+        return pltpu.make_async_remote_copy(
+            src_ref=grad_pairs.at[x_to, pl.ds(5 * z_to, 5)], dst_ref=landing.at[home, 0:5],
+            send_sem=dp_send.at[1, r], recv_sem=dp_recv.at[1, r],
+            device_id=device, device_id_type=MESH,
+        )
+
+    grads_own = pltpu.make_async_copy(
+        grad_pairs.at[x_pos, pl.ds(5 * z_hi, 5)], landing.at[home, 0:5], local_sem.at[0]
+    )
 
     tall = values[...].astype(BF16)
     for n in range(3):
@@ -257,7 +275,7 @@
     for load in loads[4:]:
         load.start()
     slab_to_owners(0, None)
-    pl.semaphore_wait(barrier, 25)
+    pl.semaphore_wait(barrier, 34)
     space_start(0)
 
     pieces[...] = jnp.zeros((TALL, 512), F32)
@@ -281,7 +299,6 @@
     space_wait(0)
     line_up_planes(0)
     along_x(modes, None)
-    gather_start(0, modes, all_modes)
     row = kz_weight[me % 2, 0:1, :]
 
     def mix_step(j, carry):
@@ -309,6 +326,9 @@
             to_in, values[:, columns].astype(BF16), (((0,), (0,)), ((), ())), preferred_element_type=F32
         )
     space_wait(1)
+    for r in far_first:
+        modes_copy(r).start()
+    all_modes[home] = modes[x_pos]
     owners_to_slab(1)
 
     full = lined[...]
@@ -358,7 +378,9 @@
     space_wait(2)
     line_up_planes(2)
     along_x(grad_modes, row)
-    gather_start(1, grad_modes, all_grads)
+    for r in far_first:
+        grads_copy(r).start()
+    grads_own.start()
 
     def grad_step(j, carry):
         strip = strip_at(j)
@@ -375,35 +397,91 @@
     planes_to_slabs(3, point)
     space_start(3)
 
-    partial8 = partial.reshape(8, 25, 4, 128)
-    gathered8 = gathered.reshape(4, 8, 25, 4, 128)
-    for r in range(1, 8):
-        gather_copy(0, modes, all_modes, r).wait()
-        gather_copy(1, grad_modes, all_grads, r).wait()
-
-    def scatter_copy(r):
-        to = (z_hi + r) % 4
-        return pltpu.make_async_remote_copy(
-            src_ref=partial8.at[to * 2 + core], dst_ref=landed.at[r - 1],
-            send_sem=dp_send.at[2, r], recv_sem=dp_recv.at[2, r],
-            device_id=(to * 8 + eight, me), device_id_type=MESH,
-        )
-
-    for r in (2, 1, 3, 0):
-        start = (z_hi + r) % 4 * 5 + 2 * core
-
-        def part_step(i, carry):
-            first, second = jnp.zeros((PAIRS, 128), F32), jnp.zeros((PAIRS, 128), F32)
-            for b in range(8):
-                slope = all_grads[b]
-                first = first + all_modes[b, pl.ds(2 * (start + i), 1), :] * slope
-                second = second + all_modes[b, pl.ds(2 * (start + i) + 1, 1), :] * slope
-            partial[start + i] = first + other(second)
-            return carry
-
-        lax.fori_loop(0, 3, part_step, 0)
-        if r != 0:
-            scatter_copy(r).start()
+    partial_pairs = partial.reshape(C, 8, 2, 128)
+    own_pairs = own_sum.reshape(10, 8, 2, 128)
+    blocks = gathered.reshape(4, C, C, 2, 128)
+    for r in far_first:
+        modes_copy(r).wait()
+        grads_copy(r).wait()
+    grads_own.wait()
+
+    def part_step(i, carry):
+        c = (i + 10 * (1 - core)) % C
+        first, second = jnp.zeros((16, 128), F32), jnp.zeros((16, 128), F32)
+        for b in range(16):
+            slope = all_grads[b]
+            first = first + all_modes[b, pl.ds(2 * c, 1), :] * slope
+            second = second + all_modes[b, pl.ds(2 * c + 1, 1), :] * slope
+        partial[c] = first + other(second)
+        return carry
+
+    core_sum = pltpu.make_async_remote_copy(
+        src_ref=partial_pairs.at[pl.ds(10 * (1 - core), 10), 0:5],
+        dst_ref=landed.reshape(10, 8, 2, 128).at[:, 0:5],
+        send_sem=dp_send.at[2, 0], recv_sem=dp_recv.at[2, 0],
+        device_id=(z_hi * 8 + x_pos * 2 + 1 - core, me), device_id_type=MESH,
+    )
+    lax.fori_loop(0, 10, part_step, 0)
+    core_sum.start()
+    lax.fori_loop(10, 20, part_step, 0)
+    core_sum.wait()
+    for j in range(10):
+        own_sum[j] = partial[10 * core + j] + landed[j]
+
+    def first_part(strip, k):
+        return blocks.at[strip, pl.ds(10 * core, SPLIT), pl.ds((z_hi - k) % 4 * 5, 5)]
+
+    def second_part(strip, k):
+        return blocks.at[strip, pl.ds(10 * core + SPLIT, 10 - SPLIT), pl.ds((z_hi - k) % 4 * 5, 5)]
+
+    own_first = own_pairs.at[0:SPLIT, 0:5]
+    own_second = own_pairs.at[SPLIT:10, 0:5]
+    keep = pltpu.make_async_copy(
+        own_pairs.at[:, 0:5], blocks.at[x_pos, pl.ds(10 * core, 10), pl.ds(5 * z_hi, 5)], local_sem.at[1]
+    )
+
+    def to_z(source, block, send_at, recv_at, r):
+        return pltpu.make_async_remote_copy(
+            src_ref=source, dst_ref=block, send_sem=send_at, recv_sem=recv_at,
+            device_id=((z_hi + r) % 4 * 8 + eight, me), device_id_type=MESH,
+        )
+
+    def to_x(source, block, send_at, recv_at, r):
+        return pltpu.make_async_remote_copy(
+            src_ref=source, dst_ref=block, send_sem=send_at, recv_sem=recv_at,
+            device_id=(z_hi * 8 + (x_pos + r) % 4 * 2 + core, me), device_id_type=MESH,
+        )
+
+    def z_copy(r):
+        return to_z(own_first, first_part(x_pos, 0), dp_send.at[4, r], dp_recv.at[4, r], r)
+
+    def x_copy(k, r):
+        block = first_part(x_pos, k)
+        return to_x(own_first if k == 0 else block, block, x_send.at[k, r], x_recv.at[k, r], r)
+
+    def x_first(r):
+        return to_x(own_second, second_part(x_pos, 0), dp_send.at[6, r], dp_recv.at[6, r], r)
+
+    def z_second(j, r):
+        block = second_part((x_pos - j) % 4, 0)
+        return to_z(own_second if j == 0 else block, block, z_send.at[j, r], z_recv.at[j, r], r)
+
+    def core_copy(k):
+        block = blocks.at[:, pl.ds(10 * core, 10), pl.ds((z_hi - k) % 4 * 5, 5)]
+        return pltpu.make_async_remote_copy(
+            src_ref=block, dst_ref=block,
+            send_sem=dp_send.at[7, k], recv_sem=dp_recv.at[7, k],
+            device_id=(z_hi * 8 + x_pos * 2 + 1 - core, me), device_id_type=MESH,
+        )
+
+    keep.start()
+    for r in (2, 1, 3):
+        x_first(r).start()
+    for r in (2, 1, 3):
+        z_copy(r).start()
+    for r in (2, 1, 3):
+        z_second(0, r).start()
+        x_copy(0, r).start()
 
     bias_total = jnp.zeros((C, 128), F32)
     for s in range(SLABS):
@@ -426,6 +504,10 @@
     for r in range(1, 8):
         eight_copy(r).start()
 
+    for j in (1, 3, 2):
+        x_first(j).wait_recv()
+        for r in (2, 1, 3):
+            z_second(j, r).start()
     full = lined[...]
     for n in range(9):
         columns = slice(256 * n, 256 * n + 256)
@@ -433,53 +515,6 @@
         for p in range(PLANES):
             grad_vmem[0, 0, p, :, columns] = result[ROWS * p : ROWS * p + C].astype(BF16)
 
-    for r in range(1, 4):
-        scatter_copy(r).wait()
-    gathered8[x_pos, z_hi * 2 + core] = partial8[z_hi * 2 + core] + landed[0] + landed[1] + landed[2]
-
-    def own(k):
-        return (z_hi - k) % 4 * 2 + core
-
-    def to_z(block, send_at, recv_at, r):
-        return pltpu.make_async_remote_copy(
-            src_ref=block, dst_ref=block, send_sem=send_at, recv_sem=recv_at,
-            device_id=((z_hi + r) % 4 * 8 + eight, me), device_id_type=MESH,
-        )
-
-    def to_x(block, send_at, recv_at, r):
-        return pltpu.make_async_remote_copy(
-            src_ref=block, dst_ref=block, send_sem=send_at, recv_sem=recv_at,
-            device_id=(z_hi * 8 + (x_pos + r) % 4 * 2 + core, me), device_id_type=MESH,
-        )
-
-    def z_copy(r):
-        return to_z(gathered8.at[x_pos, own(0), 0:SPLIT], dp_send.at[4, r], dp_recv.at[4, r], r)
-
-    def x_copy(k, r):
-        return to_x(gathered8.at[x_pos, own(k), 0:SPLIT], x_send.at[k, r], x_recv.at[k, r], r)
-
-    def x_first(r):
-        return to_x(gathered8.at[x_pos, own(0), SPLIT:25], dp_send.at[7, r], dp_recv.at[7, r], r)
-
-    def z_second(j, r):
-        return to_z(gathered8.at[(x_pos - j) % 4, own(0), SPLIT:25], z_send.at[j, r], z_recv.at[j, r], r)
-
-    def core_copy(k):
-        block = gathered8.at[:, (z_hi - k) % 4 * 2 + core]
-        return pltpu.make_async_remote_copy(
-            src_ref=block, dst_ref=block,
-            send_sem=dp_send.at[6, k], recv_sem=dp_recv.at[6, k],
-            device_id=(z_hi * 8 + x_pos * 2 + 1 - core, me), device_id_type=MESH,
-        )
-
-    for r in (2, 1, 3):
-        x_first(r).start()
-    for r in (2, 1, 3):
-        z_copy(r).start()
-    for r in (2, 1, 3):
-        z_second(0, r).start()
-        x_copy(0, r).start()
-
     for r in range(1, 8):
         eight_copy(r).wait()
     total = sums8[0]
@@ -497,10 +532,7 @@
 
     for r in range(1, 4):
         four_copy(r).start()
-    for j in (1, 3, 2):
-        x_first(j).wait_recv()
-        for r in (2, 1, 3):
-            z_second(j, r).start()
+    keep.wait()
     for k in (1, 3, 2):
         z_copy(k).wait_recv()
         for r in (2, 1, 3):
@@ -590,17 +622,19 @@
             pltpu.VMEM((ROWS, 128), F32),
             pltpu.VMEM((4, SLABS, C, 128), F32),
             pltpu.VMEM((4, SLABS, C, 128), F32),
-            pltpu.VMEM((8, PAIRS, 128), F32),
-            pltpu.VMEM((8, PAIRS, 128), F32),
-            pltpu.VMEM((C, PAIRS, 128), F32),
-            pltpu.VMEM((3, 25, 4, 128), F32),
+            pltpu.VMEM((16, PAIRS, 128), F32),
+            pltpu.VMEM((16, 16, 128), F32),
+            pltpu.VMEM((C, 16, 128), F32),
+            pltpu.VMEM((10, 16, 128), F32),
+            pltpu.VMEM((10, 16, 128), F32),
             pltpu.VMEM((8, C, 128), F32),
             pltpu.VMEM((4, C, 128), F32),
             pltpu.SemaphoreType.DMA((9,)),
+            pltpu.SemaphoreType.DMA((2,)),
             pltpu.SemaphoreType.DMA((4, 16)),
             pltpu.SemaphoreType.DMA((4, 16)),
-            pltpu.SemaphoreType.DMA((8, 8)),
-            pltpu.SemaphoreType.DMA((8, 8)),
+            pltpu.SemaphoreType.DMA((8, 16)),
+            pltpu.SemaphoreType.DMA((8, 16)),
             pltpu.SemaphoreType.DMA((4, 4)),
             pltpu.SemaphoreType.DMA((4, 4)),
             pltpu.SemaphoreType.DMA((4, 4)),

time: 73.7 us -> 73.6 us (level)
  no operation moved by 1% of the time
where the time goes in v4:
time: 73.6 us; the launch traced here: 73.4 us
  Pallas kernels  72.8 us (99%)
    pallas_call x1, Pallas kernels, on_device(): pl.pallas_call(kernel, out_shape=(pltpu.VMEM(field, BF16), pltpu.VMEM(fie...  70.6 us
    pallas_call x1, Pallas kernels, on_device(): pl.pallas_call(results, out_shape=(jax.ShapeDtypeStruct(field, BF16), jax...  2.17 us

profile of v4, /device:TPU:1, one launch (start us, length us, event | category | flops | bytes accessed | tf_op | source)
XLA Modules:
  0.0 73.4 jit_solution(16494457634274100692)
XLA Ops:
  0.6 70.6 %shard_map.137 = (bf16[1,1,3,20,2304]{4,3,2,1,0:T(8,128)(2,1)S(1)}, bf16[1,1,3,20,2304]{4,3,2,1,0:T(8,128)(2,1)S(1)}, f32[4,20,40,128]{3,2,1,0:T(8,128)S(1)}, f32[24,128]{1,0:T(8,128)S(1)}) custom-call(bf16[1,1,3,20,2304]{4,3,2,1,0:T(8,128)(2,1)} %wake_hbm.1, bf16[1,1,3,20,2304]{4,3,2,1,0:T(8,128)(2,1)} %cot_hbm.1, bf16[20,20,2,432]{3,2,1,0:T(2,128)(2,1)} %bitcast.5, ...), custom_call_target="tpu_custom_call" | custom-call | tf_op jit(solution)/shard_map/pallas_call | solution.py:593
  71.2 2.2 %shard_map.138 = (bf16[1,1,3,20,2304]{4,3,2,1,0:T(8,128)(2,1)}, bf16[1,1,3,20,2304]{4,3,2,1,0:T(8,128)(2,1)}, f32[20,20,2,512]{3,2,1,0:T(2,128)}, f32[20,20]{1,0:T(8,128)}, f32[1,20]{1,0:T(1,128)}) custom-call(bf16[1,1,3,20,2304]{4,3,2,1,0:T(8,128)(2,1)S(1)} %get-tuple-element.14.out_from, bf16[1,1,3,20,2304]{4,3,2,1,0:T(8,128)(2,1)S(1)} %get-tuple-element.15.grad_from, ...), custom_call_target="tpu_custom_call" | custom-call | tf_op jit(solution)/shard_map/pallas_call | solution.py:647

commit v5 on v4

--- a/solution.py
+++ b/solution.py
@@ -99,7 +99,7 @@
     wake_hbm, cot_hbm, weight_hbm, point_weight, bias_term, kz_weight, fwd_hbm, inv_hbm, x_hbm, xt_hbm,
     out_vmem, grad_vmem, gathered, sums_ref,
     wake, cot, weight, fwd, inv, xf, xt,
-    values, slopes, maps, spectra, slab, grads, lined, pieces, modes, mixed, grad_modes, matrix,
+    values, slopes, maps, slab, grads, lined, pieces, modes, mixed, grad_modes, matrix,
     send, recv, all_modes, all_grads, partial, landed, own_sum, sums8, sums4,
     load_sem, local_sem, send_sem, recv_sem, dp_send, dp_recv, x_send, x_recv, z_send, z_recv,
 ):
@@ -113,11 +113,13 @@
     home = z_hi * 4 + x_pos
     far_first = (8, 7, 9, 6, 10, 5, 11, 4, 12, 3, 13, 2, 14, 1, 15)
 
+    third_at = [(me + i) % 3 for i in range(3)]
+
     loads = [
         pltpu.make_async_copy(wake_hbm, wake, load_sem.at[0]),
-        pltpu.make_async_copy(fwd_hbm.at[0], fwd.at[0], load_sem.at[1]),
-        pltpu.make_async_copy(fwd_hbm.at[1], fwd.at[1], load_sem.at[2]),
-        pltpu.make_async_copy(fwd_hbm.at[2], fwd.at[2], load_sem.at[3]),
+        pltpu.make_async_copy(fwd_hbm.at[third_at[0]], fwd.at[third_at[0]], load_sem.at[1]),
+        pltpu.make_async_copy(fwd_hbm.at[third_at[1]], fwd.at[third_at[1]], load_sem.at[2]),
+        pltpu.make_async_copy(fwd_hbm.at[third_at[2]], fwd.at[third_at[2]], load_sem.at[3]),
         pltpu.make_async_copy(weight_hbm, weight, load_sem.at[4]),
         pltpu.make_async_copy(cot_hbm, cot, load_sem.at[5]),
         pltpu.make_async_copy(x_hbm, xf, load_sem.at[6]),
@@ -176,13 +178,18 @@
             total = jnp.where(where == index, part, total)
         return total
 
-    def slab_to_owners(phase, ride):
-        for t in range(TILES):
+    def slab_to_owners(phase, n, spectra, ride):
+        for t in range(2):
             held = [spectra[ROWS * p : ROWS * p + C, 128 * t : 128 * t + 128] for p in range(PLANES)]
             for k in range(3):
-                if 3 * t + k < SLABS:
-                    message = choose(slot, [(p, turn(held[p], 12 * (p - k))) for p in range(PLANES)])
-                    send[phase, 3 * t + k] = message if ride is None else message + ride
+                message = choose(slot, [(p, turn(held[p], 12 * (p - k))) for p in range(PLANES)])
+                send[phase, 6 * n + 3 * t + k] = message if ride is None else message + ride
+        for j in range(6):
+            to = 6 * n + j
+
+            @pl.when((to < SLABS) & (to != me))
+            def _():
+                space_copy(phase, (to + SLABS - me) % SLABS).start()
 
     def owners_to_slab(phase):
         for t in range(TILES):
@@ -267,16 +274,17 @@
     )
 
     tall = values[...].astype(BF16)
-    for n in range(3):
-        loads[1 + n].wait()
-        spectra[:, 256 * n : 256 * n + 256] = jnp.dot(
-            tall, fwd[n, 0], preferred_element_type=F32
-        ) + jnp.dot(tall, fwd[n, 1], preferred_element_type=F32)
+    for i, n in enumerate(third_at):
+        loads[1 + i].wait()
+        spectra = jnp.dot(tall, fwd[n, 0], preferred_element_type=F32) + jnp.dot(
+            tall, fwd[n, 1], preferred_element_type=F32
+        )
+        if i == 0:
+            pl.semaphore_wait(barrier, 34)
+        slab_to_owners(0, n, spectra, None)
     for load in loads[4:]:
         load.start()
-    slab_to_owners(0, None)
-    pl.semaphore_wait(barrier, 34)
-    space_start(0)
+    recv[0, me] = send[0, me]
 
     pieces[...] = jnp.zeros((TALL, 512), F32)
     maps[:, :, 384:] = jnp.zeros((C, PAIRS, 128), F32)
@@ -349,11 +357,11 @@
         bias_sum = bias_sum + jnp.sum(slope, axis=1, keepdims=True)
 
     full = grads[...]
-    for n in range(3):
-        spectra[:, 256 * n : 256 * n + 256] = times(full, fwd[n, 0], fwd[n, 1])
     bias_own = bias_sum[:C] + bias_sum[ROWS : ROWS + C] + bias_sum[2 * ROWS : 2 * ROWS + C]
-    slab_to_owners(2, jnp.where(lane == 108, bias_own, 0.0))
-    space_start(2)
+    ride = jnp.where(lane == 108, bias_own, 0.0)
+    for n in third_at:
+        slab_to_owners(2, n, times(full, fwd[n, 0], fwd[n, 1]), ride)
+    recv[2, me] = send[2, me]
 
     point = jnp.zeros((ROWS, ROWS), F32)
     last = (((1,), (1,)), ((), ()))
@@ -612,7 +620,6 @@
             pltpu.VMEM((TALL, CELLS), F32),
             pltpu.VMEM((C, PAIRS, 512), F32),
             pltpu.VMEM((TALL, WIDE), F32),
-            pltpu.VMEM((TALL, WIDE), F32),
             pltpu.VMEM((TALL, CELLS), F32),
             pltpu.VMEM((TALL, WIDE), F32),
             pltpu.VMEM((TALL, 512), F32),
@@ -620,7 +627,7 @@
             pltpu.VMEM((4, PAIRS, 128), F32),
             pltpu.VMEM((4, PAIRS, 128), F32),
             pltpu.VMEM((ROWS, 128), F32),
-            pltpu.VMEM((4, SLABS, C, 128), F32),
+            pltpu.VMEM((4, 3 * TILES, C, 128), F32),
             pltpu.VMEM((4, SLABS, C, 128), F32),
             pltpu.VMEM((16, PAIRS, 128), F32),
             pltpu.VMEM((16, 16, 128), F32),

time: 73.6 us -> 74 us (level)
  no operation moved by 1% of the time
where the time goes in v5:
time: 74 us; the launch traced here: 73.8 us
  Pallas kernels  73.2 us (99%)
    pallas_call x1, Pallas kernels, on_device(): pl.pallas_call(kernel, out_shape=(pltpu.VMEM(field, BF16), pltpu.VMEM(fie...  71 us
    pallas_call x1, Pallas kernels, on_device(): pl.pallas_call(results, out_shape=(jax.ShapeDtypeStruct(field, BF16), jax...  2.17 us

profile of v5, /device:TPU:1, one launch (start us, length us, event | category | flops | bytes accessed | tf_op | source)
XLA Modules:
  0.0 73.8 jit_solution(14682887665152719154)
XLA Ops:
  0.6 71.0 %shard_map.137 = (bf16[1,1,3,20,2304]{4,3,2,1,0:T(8,128)(2,1)S(1)}, bf16[1,1,3,20,2304]{4,3,2,1,0:T(8,128)(2,1)S(1)}, f32[4,20,40,128]{3,2,1,0:T(8,128)S(1)}, f32[24,128]{1,0:T(8,128)S(1)}) custom-call(bf16[1,1,3,20,2304]{4,3,2,1,0:T(8,128)(2,1)} %wake_hbm.1, bf16[1,1,3,20,2304]{4,3,2,1,0:T(8,128)(2,1)} %cot_hbm.1, bf16[20,20,2,432]{3,2,1,0:T(2,128)(2,1)} %bitcast.5, ...), custom_call_target="tpu_custom_call" | custom-call | tf_op jit(solution)/shard_map/pallas_call | solution.py:601
  71.7 2.2 %shard_map.138 = (bf16[1,1,3,20,2304]{4,3,2,1,0:T(8,128)(2,1)}, bf16[1,1,3,20,2304]{4,3,2,1,0:T(8,128)(2,1)}, f32[20,20,2,512]{3,2,1,0:T(2,128)}, f32[20,20]{1,0:T(8,128)}, f32[1,20]{1,0:T(1,128)}) custom-call(bf16[1,1,3,20,2304]{4,3,2,1,0:T(8,128)(2,1)S(1)} %get-tuple-element.14.out_from, bf16[1,1,3,20,2304]{4,3,2,1,0:T(8,128)(2,1)S(1)} %get-tuple-element.15.grad_from, ...), custom_call_target="tpu_custom_call" | custom-call | tf_op jit(solution)/shard_map/pallas_call | solution.py:654

commit v6 on v4

--- a/solution.py
+++ b/solution.py
@@ -462,9 +462,9 @@
     def x_first(r):
         return to_x(own_second, second_part(x_pos, 0), dp_send.at[6, r], dp_recv.at[6, r], r)
 
-    def z_second(j, r):
-        block = second_part((x_pos - j) % 4, 0)
-        return to_z(own_second if j == 0 else block, block, z_send.at[j, r], z_recv.at[j, r], r)
+    def z_second(r):
+        block = blocks.at[:, pl.ds(10 * core + SPLIT, 10 - SPLIT), pl.ds(5 * z_hi, 5)]
+        return to_z(block, block, z_send.at[r], z_recv.at[r], r)
 
     def core_copy(k):
         block = blocks.at[:, pl.ds(10 * core, 10), pl.ds((z_hi - k) % 4 * 5, 5)]
@@ -480,7 +480,6 @@
     for r in (2, 1, 3):
         z_copy(r).start()
     for r in (2, 1, 3):
-        z_second(0, r).start()
         x_copy(0, r).start()
 
     bias_total = jnp.zeros((C, 128), F32)
@@ -504,10 +503,11 @@
     for r in range(1, 8):
         eight_copy(r).start()
 
-    for j in (1, 3, 2):
-        x_first(j).wait_recv()
-        for r in (2, 1, 3):
-            z_second(j, r).start()
+    keep.wait()
+    for r in (1, 3, 2):
+        x_first(r).wait_recv()
+    for r in (2, 1, 3):
+        z_second(r).start()
     full = lined[...]
     for n in range(9):
         columns = slice(256 * n, 256 * n + 256)
@@ -515,6 +515,11 @@
         for p in range(PLANES):
             grad_vmem[0, 0, p, :, columns] = result[ROWS * p : ROWS * p + C].astype(BF16)
 
+    for k in (1, 3):
+        z_copy(k).wait_recv()
+        for r in (2, 1, 3):
+            x_copy(k, r).start()
+
     for r in range(1, 8):
         eight_copy(r).wait()
     total = sums8[0]
@@ -532,18 +537,15 @@
 
     for r in range(1, 4):
         four_copy(r).start()
-    keep.wait()
-    for k in (1, 3, 2):
-        z_copy(k).wait_recv()
-        for r in (2, 1, 3):
-            x_copy(k, r).start()
+    z_copy(2).wait_recv()
+    for r in (2, 1, 3):
+        x_copy(2, r).start()
     order = (0, 1, 3, 2)
     for k in order:
         for r in range(1, 4):
             x_copy(k, r).wait_recv()
         if k != 0:
-            for j in range(4):
-                z_second(j, k).wait_recv()
+            z_second(k).wait_recv()
         core_copy(k).start()
     for r in range(1, 4):
         four_copy(r).wait()
@@ -554,8 +556,7 @@
     for r in range(1, 4):
         z_copy(r).wait_send()
         x_first(r).wait_send()
-        for j in range(4):
-            z_second(j, r).wait_send()
+        z_second(r).wait_send()
         for k in range(4):
             x_copy(k, r).wait_send()
     for k in order:
@@ -637,8 +638,8 @@
             pltpu.SemaphoreType.DMA((8, 16)),
             pltpu.SemaphoreType.DMA((4, 4)),
             pltpu.SemaphoreType.DMA((4, 4)),
-            pltpu.SemaphoreType.DMA((4, 4)),
-            pltpu.SemaphoreType.DMA((4, 4)),
+            pltpu.SemaphoreType.DMA((4,)),
+            pltpu.SemaphoreType.DMA((4,)),
         ],
         compiler_params=pltpu.CompilerParams(
             collective_id=0, has_side_effects=True, vmem_limit_bytes=52 * 1024 * 1024

time: 73.6 us -> 73.5 us (level)
  no operation moved by 1% of the time
where the time goes in v6:
time: 73.5 us; the launch traced here: 73.3 us
  Pallas kernels  72.7 us (99%)
    pallas_call x1, Pallas kernels, on_device(): pl.pallas_call(kernel, out_shape=(pltpu.VMEM(field, BF16), pltpu.VMEM(fie...  70.5 us
    pallas_call x1, Pallas kernels, on_device(): pl.pallas_call(results, out_shape=(jax.ShapeDtypeStruct(field, BF16), jax...  2.17 us

profile of v6, /device:TPU:1, one launch (start us, length us, event | category | flops | bytes accessed | tf_op | source)
XLA Modules:
  0.0 73.3 jit_solution(14793159186243690289)
XLA Ops:
  0.6 70.5 %shard_map.137 = (bf16[1,1,3,20,2304]{4,3,2,1,0:T(8,128)(2,1)S(1)}, bf16[1,1,3,20,2304]{4,3,2,1,0:T(8,128)(2,1)S(1)}, f32[4,20,40,128]{3,2,1,0:T(8,128)S(1)}, f32[24,128]{1,0:T(8,128)S(1)}) custom-call(bf16[1,1,3,20,2304]{4,3,2,1,0:T(8,128)(2,1)} %wake_hbm.1, bf16[1,1,3,20,2304]{4,3,2,1,0:T(8,128)(2,1)} %cot_hbm.1, bf16[20,20,2,432]{3,2,1,0:T(2,128)(2,1)} %bitcast.5, ...), custom_call_target="tpu_custom_call" | custom-call | tf_op jit(solution)/shard_map/pallas_call | solution.py:594
  71.1 2.2 %shard_map.138 = (bf16[1,1,3,20,2304]{4,3,2,1,0:T(8,128)(2,1)}, bf16[1,1,3,20,2304]{4,3,2,1,0:T(8,128)(2,1)}, f32[20,20,2,512]{3,2,1,0:T(2,128)}, f32[20,20]{1,0:T(8,128)}, f32[1,20]{1,0:T(1,128)}) custom-call(bf16[1,1,3,20,2304]{4,3,2,1,0:T(8,128)(2,1)S(1)} %get-tuple-element.14.out_from, bf16[1,1,3,20,2304]{4,3,2,1,0:T(8,128)(2,1)S(1)} %get-tuple-element.15.grad_from, ...), custom_call_target="tpu_custom_call" | custom-call | tf_op jit(solution)/shard_map/pallas_call | solution.py:648
